TPU v7x, 32 devices: a whole 2x2x4 slice. The times are simulated.
32 devices in a mesh: dp: 16 (over z, y, core), mp: 2 (over x).
Axes of the slice: x: 2, y: 2, z: 4, core: 2. Of those that a mesh axis runs over, the one named last changes fastest.
Arguments:
- inputs: bfloat16 [2, 4096, 2048], P(None, 'dp'), may hold values from -6 to 6
- seq_starts: int32 [2, 4096], P(None, 'dp'), may hold values from 0 to 4095, as said below
- cotangent: bfloat16 [2, 4096, 2048], P(None, 'dp'), may hold values from -6 to 6
- attn_gain: bfloat16 [2048], P('dp'), may hold values from 0.5 to 1.5
- query_weight: bfloat16 [2048, 2048], P('dp', 'mp'), may hold values from -0.125 to 0.125
- key_matrix: bfloat16 [2048, 512], P('dp', 'mp'), may hold values from -0.125 to 0.125
- value_matrix: bfloat16 [2048, 512], P('dp', 'mp'), may hold values from -0.125 to 0.125
- out_weight: bfloat16 [2048, 2048], P('mp', 'dp'), may hold values from -0.5 to 0.5
- mlp_gain: bfloat16 [2048], P('dp'), may hold values from 0.5 to 1.5
- gate_weight: bfloat16 [2048, 8192], P('dp', 'mp'), may hold values from -0.125 to 0.125
- up_weight: bfloat16 [2048, 8192], P('dp', 'mp'), may hold values from -0.125 to 0.125
- down_weight: bfloat16 [8192, 2048], P('mp', 'dp'), may hold values from -0.125 to 0.125
Outputs:
- output: bfloat16 [2, 4096, 2048], P(None, 'dp')
- input_grad: float32 [2, 4096, 2048], P(None, 'dp')
- grad_attn_gain: float32 [2048], P('dp')
- grad_query: float32 [2048, 2048], P('dp', 'mp')
- grad_key: float32 [2048, 512], P('dp', 'mp')
- grad_value: float32 [2048, 512], P('dp', 'mp')
- grad_out: float32 [2048, 2048], P('mp', 'dp')
- grad_mlp_gain: float32 [2048], P('dp')
- grad_gate: float32 [2048, 8192], P('dp', 'mp')
- grad_up: float32 [2048, 8192], P('dp', 'mp')
- grad_down: float32 [8192, 2048], P('mp', 'dp')
Inputs may be any that keep to these rules, and one draw needn't show every extreme that they name: `seq_starts`: each entry is the index, within its micro-batch of 4096 tokens, of the first token of its sequence: entries never fall along a micro-batch, never exceed their own index, every multiple of 256 begins a sequence, and the last token of a micro-batch begins a sequence of its own.
All inputs are finite; a program needn't handle non-finite values.
Results may differ from a plain program's by a relative error of at most 0.015.
Values may be sent and summed in bfloat16 or wider, within the bound.
No kernel may reach another device: no remote copies, remote signals or barrier semaphores. Data moves between devices by JAX's collectives and lax.ppermute only.
A program may use at most 320 MiB of HBM per device.

v0:
```python
import functools
import math

import jax
import jax.numpy as jnp
from jax import lax
from jax.experimental import pallas as pl
from jax.experimental.pallas import tpu as pltpu
from jax.sharding import PartitionSpec as P

HEAD_SIZE = 64
LANES = 2 * HEAD_SIZE
EPSILON = 1e-05
F32 = jnp.float32
BF16 = jnp.bfloat16
PIECES = 4
VMEM_LIMIT = 56 << 20
TIME_BYTES = 1_000


def dot(left, right, left_dim, right_dim):
    return lax.dot_general(
        left, right, (((left_dim,), (right_dim,)), ((), ())), preferred_element_type=F32
    )


def add_low(left, right):
    return (left.astype(F32) + right.astype(F32)).astype(BF16)


def rope_tables(positions):
    halfway = HEAD_SIZE // 2
    lane = jnp.arange(LANES, dtype=jnp.int32)
    frequency = 500000.0 ** (-((lane % halfway).astype(F32) * 2.0 / HEAD_SIZE))
    angles = positions.astype(F32)[..., None] * frequency
    sign = jnp.where(lane % HEAD_SIZE < halfway, -1.0, 1.0)
    return (jnp.cos(angles), jnp.sin(angles) * sign)


def kernel_call(kernel, grid, ins, outs, scalars=(), scratch=(), time=2, into=()):
    first = len(scalars) + len(ins)

    def spec(array, block, place):
        single = tuple(block) == array.shape or place.__name__ == "fixed"
        mode = pl.Buffered(1) if single and math.prod(grid) > 1 else None
        return pl.BlockSpec(block, place, pipeline_mode=mode)
    return pl.pallas_call(
        kernel,
        grid_spec=pltpu.PrefetchScalarGridSpec(
            num_scalar_prefetch=len(scalars),
            grid=grid,
            in_specs=[spec(*entry) for entry in ins]
            + [pl.BlockSpec(memory_space=pl.ANY)] * len(into),
            out_specs=[pl.BlockSpec(block, place) for _, _, block, place in outs],
            scratch_shapes=list(scratch),
        ),
        out_shape=[jax.ShapeDtypeStruct(shape, kind) for shape, kind, _, _ in outs],
        compiler_params=pltpu.CompilerParams(vmem_limit_bytes=VMEM_LIMIT),
        cost_estimate=pl.CostEstimate(
            flops=1, bytes_accessed=int(time * TIME_BYTES), transcendentals=0
        ),
        input_output_aliases={first + i: i for i in range(len(into))},
    )(*scalars, *[array for array, _, _ in ins], *into)


def whole(array):
    return (array, array.shape, lambda *_: (0,) * array.ndim)


def by_rows(array, rows):
    return (array, (rows,) + array.shape[1:], lambda i, *_: (i,) + (0,) * (array.ndim - 1))


def by_columns(array, columns, first=0):
    return (array, (array.shape[0], columns), lambda j, *_: (0, j + first))


def turn_lanes(pair_rows):
    lane = lax.broadcasted_iota(jnp.int32, pair_rows.shape, 1)
    up = pltpu.roll(pair_rows, LANES - HEAD_SIZE // 2, 1)
    down = pltpu.roll(pair_rows, HEAD_SIZE // 2, 1)
    return jnp.where(lane % HEAD_SIZE < HEAD_SIZE // 2, up, down)


def doubled(pair_rows, second):
    lane = lax.broadcasted_iota(jnp.int32, pair_rows.shape, 1)
    other = pltpu.roll(pair_rows, HEAD_SIZE, 1)
    return jnp.where((lane < HEAD_SIZE) != second, pair_rows, other)


def half_lanes(pair_rows, second):
    lane = lax.broadcasted_iota(jnp.int32, pair_rows.shape, 1)
    return jnp.where((lane < HEAD_SIZE) != second, pair_rows, jnp.zeros_like(pair_rows))


def allowed_pairs(start_col_ref, start_row_ref):
    rows = start_col_ref.shape[1]
    shape = (rows, rows)
    before = lax.broadcasted_iota(jnp.int32, shape, 1) <= lax.broadcasted_iota(jnp.int32, shape, 0)
    return (start_col_ref[0] == start_row_ref[0]) & before


def head_probs(query, key, allowed):
    scores = dot(query, key, 1, 1) * (1.0 / math.sqrt(HEAD_SIZE))
    scores = jnp.where(allowed, scores, -1e30)
    expo = jnp.exp(scores - jnp.max(scores, axis=-1, keepdims=True))
    return expo / jnp.sum(expo, axis=-1, keepdims=True)


def times_pieces(left, refs, columns):
    total = None
    depth = refs[0].shape[0]
    for p, ref in enumerate(refs):
        part = dot(left[:, p * depth : (p + 1) * depth], ref[:, :columns], 1, 0)
        total = part if total is None else total + part
    return total


def attend(q_cols, k_cols, raw_ref, cosine, sine, allowed, rot_ref, out_ref):
    group_width = q_cols // k_cols

    def rope(at):
        rows = raw_ref[:, at : at + LANES]
        return (rows * cosine + turn_lanes(rows) * sine).astype(BF16)

    for kv in range(k_cols // LANES):
        k_at, v_at = q_cols + kv * LANES, q_cols + k_cols + kv * LANES
        key = rope(k_at)
        value = raw_ref[:, v_at : v_at + LANES].astype(BF16)
        rot_ref[:, k_at : k_at + LANES] = key
        rot_ref[:, v_at : v_at + LANES] = value
        for group in (0, 1):
            key_two, value_two = doubled(key, group == 1), doubled(value, group == 1)
            for pair in range(group_width // 2):
                at = ((kv * 2 + group) * group_width + 2 * pair) * HEAD_SIZE
                query = rope(at)
                rot_ref[:, at : at + LANES] = query
                parts = []
                for second in (False, True):
                    probs = head_probs(half_lanes(query, second), key_two, allowed)
                    parts.append(dot(probs.astype(BF16), value_two, 1, 0))
                lane = lax.broadcasted_iota(jnp.int32, parts[0].shape, 1)
                out_ref[:, at : at + LANES] = jnp.where(lane < HEAD_SIZE, *parts).astype(BF16)


def attend_back(q_cols, k_cols, rot_ref, grad_ref, cosine, sine, allowed, out_ref):
    group_width = q_cols // k_cols
    scale = 1.0 / math.sqrt(HEAD_SIZE)

    def unrope(rows):
        return (rows * cosine - turn_lanes(rows) * sine).astype(BF16)

    def folded(rows):
        return rows + pltpu.roll(rows, HEAD_SIZE, 1)

    for kv in range(k_cols // LANES):
        k_at, v_at = q_cols + kv * LANES, q_cols + k_cols + kv * LANES
        key, value = rot_ref[:, k_at : k_at + LANES], rot_ref[:, v_at : v_at + LANES]
        grad_keys, grad_values = [], []
        for group in (0, 1):
            key_two, value_two = doubled(key, group == 1), doubled(value, group == 1)
            grad_key = jnp.zeros(key.shape, F32)
            grad_value = jnp.zeros(key.shape, F32)
            for pair in range(group_width // 2):
                at = ((kv * 2 + group) * group_width + 2 * pair) * HEAD_SIZE
                query, grad = rot_ref[:, at : at + LANES], grad_ref[:, at : at + LANES]
                parts = []
                for second in (False, True):
                    query_one, grad_one = half_lanes(query, second), half_lanes(grad, second)
                    probs = head_probs(query_one, key_two, allowed)
                    grad_probs = dot(grad_one, value_two, 1, 1)
                    inner = jnp.sum(probs * grad_probs, axis=-1, keepdims=True)
                    grad_scores = (probs * (grad_probs - inner)).astype(BF16)
                    parts.append(dot(grad_scores, key_two, 1, 0))
                    grad_key = grad_key + dot(grad_scores, query_one, 0, 0)
                    grad_value = grad_value + dot(probs.astype(BF16), grad_one, 0, 0)
                lane = lax.broadcasted_iota(jnp.int32, parts[0].shape, 1)
                out_ref[:, at : at + LANES] = unrope(jnp.where(lane < HEAD_SIZE, *parts) * scale)
            grad_keys.append(folded(grad_key) * scale)
            grad_values.append(folded(grad_value))
        lane = lax.broadcasted_iota(jnp.int32, key.shape, 1)
        out_ref[:, k_at : k_at + LANES] = unrope(jnp.where(lane < HEAD_SIZE, *grad_keys))
        out_ref[:, v_at : v_at + LANES] = jnp.where(lane < HEAD_SIZE, *grad_values).astype(BF16)


def move_rows(table_ref, count, in_ref, store):
    block = in_ref.shape[-1] // count
    for p in range(count):
        at = pl.multiple_of(table_ref[p] * block, block)
        store(p * block, in_ref[0, :, pl.ds(at, block)])


def move_kernel(count, table_ref, in_ref, *refs):
    out_ref = refs[-1]

    def store(at, rows):
        out_ref[0, :, at : at + rows.shape[1]] = rows.astype(out_ref.dtype)

    move_rows(table_ref, count, in_ref, store)


def move_blocks(array, table, mine, kind, into=None, first=0):
    micro_count, rows, width = array.shape
    count = table.shape[0]
    block = width // count
    if block % 128:
        array = jnp.roll(array, -mine, axis=0)
        pieces = [
            lax.dynamic_slice_in_dim(array, table[p] * block, block, 2) for p in range(count)
        ]
        array = jnp.concatenate(pieces, axis=-1).astype(kind)
        if into is None:
            return array
        return lax.dynamic_update_slice_in_dim(into, array, first, 0)
    shape = array.shape if into is None else into.shape
    return kernel_call(
        functools.partial(move_kernel, count),
        (micro_count,),
        [(array, (1, rows, width), lambda i, t: ((i + t[count]) % micro_count, 0, 0))],
        [(shape, kind, (1, rows, width), lambda i, t: (i + first, 0, 0))],
        scalars=(jnp.concatenate([table, mine[None]]),),
        into=() if into is None else (into,),
    )[0]


def attend_kernel(count, q_cols, k_cols, table_ref, in_ref, *refs):
    weights, lasts, refs = refs[:PIECES], refs[PIECES : 2 * PIECES], refs[2 * PIECES :]
    cos_ref, sin_ref, col_ref, row_ref = refs[:4]
    rows_ref, hidden_ref, rot_ref, out_ref, gains_ref, raw_ref = refs[4:]
    step = pl.program_id(0)
    columns = q_cols + 2 * k_cols
    depth, cut = weights[0].shape

    @pl.when(step == 0)
    def _():
        shape = (8, 128)
        pick = lax.broadcasted_iota(jnp.int32, shape, 0) == lax.broadcasted_iota(jnp.int32, shape, 1)
        for p, ref in enumerate(lasts):
            gains_ref[:, p * depth : (p + 1) * depth] = dot(
                pick.astype(F32).astype(BF16), ref[:, columns - cut :], 1, 1
            )

    def store(at, rows):
        rows_ref[:, at : at + rows.shape[1]] = rows

    if count:
        move_rows(table_ref, count, in_ref, store)
    else:
        rows_ref[...] = in_ref[0]
    rows = rows_ref[...].astype(F32)
    inverse = lax.rsqrt(jnp.mean(rows * rows, axis=-1, keepdims=True) + EPSILON)
    hidden = (rows * inverse * gains_ref[0:1, :]).astype(BF16)
    hidden_ref[...] = hidden
    raw_ref[:, :cut] = times_pieces(hidden, weights, cut)
    raw_ref[:, cut:] = times_pieces(hidden, lasts, columns - cut)
    attend(
        q_cols,
        k_cols,
        raw_ref,
        cos_ref[...],
        sin_ref[...],
        allowed_pairs(col_ref, row_ref),
        rot_ref,
        out_ref,
    )


def attend_back_kernel(q_cols, k_cols, branch_ref, *refs):
    outs, refs = refs[:PIECES], refs[PIECES:]
    weights, lasts, refs = refs[:PIECES], refs[PIECES : 2 * PIECES], refs[2 * PIECES :]
    rot_ref, cos_ref, sin_ref, col_ref, row_ref = refs[:5]
    all_ref, qkv_ref, one_ref, grad_ref = refs[-4:]
    columns = q_cols + 2 * k_cols
    all_ref[...] = branch_ref[...]
    grad_ref[...] = times_pieces(branch_ref[...], outs, q_cols).astype(BF16)
    attend_back(
        q_cols,
        k_cols,
        rot_ref,
        grad_ref,
        cos_ref[...],
        sin_ref[...],
        allowed_pairs(col_ref, row_ref),
        qkv_ref,
    )
    depth, cut = weights[0].shape
    for p, (ref, last) in enumerate(zip(weights, lasts)):
        one = dot(qkv_ref[:, :cut], ref[...], 1, 1)
        one = one + dot(qkv_ref[:, cut:], last[:, : columns - cut], 1, 1)
        one_ref[:, p * depth : (p + 1) * depth] = one.astype(BF16)


def gate_kernel(*refs):
    blocks, weights, (all_ref, gate_ref) = refs[:4], refs[4 : 4 + PIECES], refs[4 + PIECES :]

    @pl.when(pl.program_id(0) == 0)
    def _():
        rows = blocks[0].shape[0]
        for i, ref in enumerate(blocks):
            all_ref[i * rows : (i + 1) * rows, :] = ref[...]

    gate_ref[...] = times_pieces(all_ref[...], weights, gate_ref.shape[1]).astype(BF16)


def up_kernel(all_ref, *refs):
    weights, (gate_ref, up_ref, mixed_ref) = refs[:PIECES], refs[PIECES:]
    up = times_pieces(all_ref[...], weights, up_ref.shape[1])
    gate = gate_ref[...].astype(F32)
    up_ref[...] = up.astype(BF16)
    mixed_ref[...] = (gate * jax.nn.sigmoid(gate) * up).astype(BF16)


def mixed_back_kernel(cot_ref, *refs):
    weights, refs = refs[:PIECES], refs[PIECES:]
    (gate_ref, up_ref), (grad_gate_ref, grad_up_ref) = refs[:2], refs[-2:]
    grad = times_pieces(cot_ref[...], weights, gate_ref.shape[1])
    gate = gate_ref[...].astype(F32)
    sigmoid = jax.nn.sigmoid(gate)
    inner = sigmoid * (1.0 + gate * (1.0 - sigmoid))
    grad_gate_ref[...] = (grad * up_ref[...].astype(F32) * inner).astype(BF16)
    grad_up_ref[...] = (grad * (gate * sigmoid)).astype(BF16)


def back_kernel(per_piece, sides, *refs):
    lefts, refs = refs[:sides], refs[sides:]
    weights, outs = refs[: sides * PIECES], refs[sides * PIECES :]
    rows = outs[0].shape[0]
    for p in range(PIECES):

        @pl.when(pl.program_id(0) // per_piece == p)
        def _(p=p):
            total = None
            for s in range(sides):
                part = dot(lefts[s][...], weights[s * PIECES + p][...], 1, 1)
                total = part if total is None else total + part
            total = total.astype(BF16)
            outs[0][...] = total[:rows]
            if len(outs) == 2:
                outs[1][...] = total[rows:]
                return
            mp_one, pair_one, mp_two, pair_two = outs[1:]
            middle = rows // 2
            mp_two[...] = total[rows : rows + middle]
            mp_one[:middle, :] = total[rows + middle : 2 * rows]
            pair_one[:middle, :] = total[2 * rows : 2 * rows + middle]
            pair_two[...] = total[2 * rows + middle : 3 * rows]
            pair_one[middle:, :] = total[3 * rows : 3 * rows + middle]
            mp_one[middle:, :] = total[3 * rows + middle :]


def times_back(sides, rows):
    depth = sides[0][1][0].shape[0]
    columns = min(depth, 512)
    per_piece = depth // columns
    ins = []
    for left, pieces, *place in sides:
        at = (0, place[0] if place else 0)

        def fixed(j, at=at):
            return at

        ins.append((left, (left.shape[0], pieces[0].shape[1]), fixed))
    for _, pieces, *_ in sides:
        for p, piece in enumerate(pieces):

            def place(j, p=p):
                return (jnp.clip(j - p * per_piece, 0, per_piece - 1), 0)

            ins.append((piece, (columns, piece.shape[1]), place))
    heights = (rows, rows, rows, rows // 2, rows // 2)
    if sides[0][0].shape[0] == 2 * rows:
        heights = (rows, rows)
    return kernel_call(
        functools.partial(back_kernel, per_piece, len(sides)),
        (PIECES * per_piece,),
        ins,
        [((h, depth * PIECES), BF16, (h, columns), lambda j: (0, j)) for h in heights],
        time=7 * len(sides) * sides[0][0].shape[1] / 1024,
    )


def forward_norm_kernel(rows_ref, own_ref, other_ref, gains_ref, after_ref, hidden_ref):
    branch = own_ref[...].astype(F32) + other_ref[...].astype(F32)
    result = rows_ref[...].astype(F32) + branch
    after_ref[...] = result
    square = jnp.mean(result * result, axis=-1, keepdims=True)
    normed = result * lax.rsqrt(square + EPSILON)
    hidden_ref[...] = (normed * gains_ref[1:2, :]).astype(BF16)


def add_kernel(rows_ref, own_ref, pair_one, mp_two, mp_one, pair_two, out_ref):
    step = pl.program_id(0)
    for i, extra in enumerate(((pair_one, mp_two), (mp_one, pair_two))):

        @pl.when(step == i)
        def _(extra=extra):
            branch = own_ref[...].astype(F32)
            branch = branch + (extra[0][...].astype(F32) + extra[1][...].astype(F32))
            out_ref[...] = (rows_ref[...].astype(F32) + branch).astype(BF16)


def norm_back_kernel(gain_row, values_ref, passed_ref, *refs):
    own_ref, pair_one, mp_two, mp_one, pair_two, gains_ref = refs[:6]
    full_ref, low_ref, gain_ref = refs[6:]
    step = pl.program_id(0)

    @pl.when(step == 0)
    def _():
        gain_ref[...] = jnp.zeros_like(gain_ref)

    for i, extra in enumerate(((pair_one, mp_two), (mp_one, pair_two))):

        @pl.when(step == i)
        def _(extra=extra):
            grad = own_ref[...].astype(F32)
            grad = grad + (extra[0][...].astype(F32) + extra[1][...].astype(F32))
            values = values_ref[...].astype(F32)
            square = jnp.mean(values * values, axis=-1, keepdims=True)
            inverse = lax.rsqrt(square + EPSILON)
            normed = values * inverse
            scaled = grad * gains_ref[gain_row : gain_row + 1, :]
            inner = jnp.mean(scaled * normed, axis=-1, keepdims=True)
            result = passed_ref[...].astype(F32) + inverse * (scaled - normed * inner)
            full_ref[...] = result
            low_ref[...] = result.astype(BF16)
            gain_ref[0:1, :] += jnp.sum(grad * normed, axis=0, keepdims=True)


def last_norm_back_kernel(count, table_ref, values_ref, passed_ref, *refs):
    parts, others, gains_ref, out_ref, gain_ref, rows_ref = refs[:2], refs[2:4], *refs[4:]
    step = pl.program_id(0)

    @pl.when(step == 0)
    def _():
        gain_ref[...] = jnp.zeros_like(gain_ref)

    for i in (0, 1):

        @pl.when(step // 2 == i)
        def _(i=i):
            grad = parts[i][...].astype(F32) + others[i][...].astype(F32)
            values = values_ref[...].astype(F32)
            square = jnp.mean(values * values, axis=-1, keepdims=True)
            inverse = lax.rsqrt(square + EPSILON)
            normed = values * inverse
            scaled = grad * gains_ref[0:1, :]
            inner = jnp.mean(scaled * normed, axis=-1, keepdims=True)
            result = passed_ref[...].astype(F32) + inverse * (scaled - normed * inner)
            rows_ref[0, :, :] = result
            gain_ref[0:1, :] += jnp.sum(grad * normed, axis=0, keepdims=True)

    def store(at, rows):
        out_ref[0, :, at : at + rows.shape[1]] = rows

    if count:
        move_rows(table_ref, count, rows_ref, store)
    else:
        out_ref[...] = rows_ref[...]


def send_kernel(left_ref, right_ref, *refs):
    refs[-1][...] = dot(left_ref[...], right_ref[...], 0, 0).astype(BF16)


def keep_kernel(left_ref, right_ref, other_ref, *refs):
    low_ref, high_ref = refs[-2:]
    total = dot(left_ref[...], right_ref[...], 0, 0) + other_ref[...].astype(F32)
    middle = low_ref.shape[0]
    low_ref[...] = total[:middle].astype(BF16)
    high_ref[...] = total[middle:].astype(BF16)


def transpose_kernel(in_ref, out_ref):
    out_ref[...] = in_ref[...].T


def transposed(array):
    rows, columns = array.shape
    if columns % 128:
        return array.T
    return kernel_call(
        transpose_kernel,
        (rows // 512,),
        [(array, (512, columns), lambda i: (i, 0))],
        [((columns, rows), array.dtype, (columns, 512), lambda i: (0, i))],
    )[0]


def owned_kernel(flip, halves, ins, *refs):
    out_ref = refs[-1]
    for i, ref in enumerate(refs[:ins]):
        parts = [ref[k].astype(F32) for k in range(4)]
        if not halves:
            total = (parts[0] + parts[2]) + (parts[1] + parts[3])
            out_ref[...] = total.T if flip else total
            return

        for side in (0, 1):

            @pl.when(pl.program_id(0) == side * ins + i)
            def _(parts=parts, side=side):
                total = parts[side] + parts[side + 2]
                out_ref[...] = total.T if flip else total


def owned(array, second, block, halves, flip):
    arrays = [a.reshape(4, block, a.shape[1]) for a in (array, second) if a is not None]
    if block % 128:
        sides = [[], []]
        for a in arrays:
            parts = a.astype(F32)
            sides[0].append(parts[0] + parts[2])
            sides[1].append(parts[1] + parts[3])
        total = [jnp.concatenate(side, axis=1) for side in sides]
        total = jnp.concatenate(total, axis=1) if halves else total[0] + total[1]
        return total.T if flip else total
    columns = arrays[0].shape[2]
    count = 2 * len(arrays) if halves else 1
    shape, part, place = (block, columns * count), (block, columns), lambda j: (0, j)
    if flip:
        shape, part, place = shape[::-1], part[::-1], lambda j: (j, 0)
    return kernel_call(
        functools.partial(owned_kernel, flip, halves, len(arrays)),
        (count,),
        [whole(a) for a in arrays],
        [(shape, F32, part, place)],
        time=3,
    )[0]


def owned_columns_kernel(cuts, one_ref, two_ref, out_ref, query_ref, key_ref, value_ref):
    one, two = (
        (ref[0].astype(F32) + ref[2].astype(F32)) + (ref[1].astype(F32) + ref[3].astype(F32))
        for ref in (one_ref, two_ref)
    )
    queries, rest, keys = cuts
    out_ref[...] = one[:, :queries].T
    query_ref[:, :rest] = one[:, queries:]
    query_ref[:, rest:] = two[:, : queries - rest]
    key_ref[...] = two[:, queries - rest : queries - rest + keys]
    value_ref[...] = two[:, queries - rest + keys :]


def owned_columns(one, two, block, cuts):
    one, two = (a.reshape(4, block, a.shape[1]) for a in (one, two))
    queries, rest, keys = cuts
    if block % 128:
        one, two = (jnp.sum(a.astype(F32), axis=0) for a in (one, two))
        together = jnp.concatenate([one, two], axis=1)
        parts = jnp.split(together, [queries, 2 * queries, 2 * queries + keys], axis=1)
        return [parts[0].T, *parts[1:]]
    shapes = [(queries, block), (block, queries), (block, keys), (block, keys)]
    return kernel_call(
        functools.partial(owned_columns_kernel, cuts),
        (1,),
        [whole(one), whole(two)],
        [(shape, F32, shape, lambda i: (0, 0)) for shape in shapes],
    )


def after(array, *earlier):
    return lax.optimization_barrier((array, *earlier))[0]


def make_per_device(n):
    pair = 4 if n <= 16 else 8
    others = [1 << b for b in reversed(range(n.bit_length() - 1))]
    others = [v for v in others if v not in (pair, 2 * pair)]
    main_order = [pair, 2 * pair] + others
    z_groups = [[i | z * pair for z in range(4)] for i in range(n) if not i & (3 * pair)]

    def swap(array, bit):
        return lax.ppermute(array, "dp", [(i, i ^ bit) for i in range(n)])

    def swap_mp(array):
        return lax.ppermute(array, "mp", [(0, 1), (1, 0)])

    def along_z(array):
        return lax.all_to_all(array, "dp", 0, 0, axis_index_groups=z_groups, tiled=True)

    def per_device(
        inputs,
        seq_starts,
        cotangent,
        attn_gain,
        query_weight,
        key_matrix,
        value_matrix,
        out_weight,
        mlp_gain,
        gate_weight,
        up_weight,
        down_weight,
    ):
        micro_count, rows, width = inputs.shape
        middle = rows // 2
        block = width // n
        tokens, pair_tokens = micro_count * rows, 2 * micro_count * rows
        q_cols, k_cols = query_weight.shape[1], key_matrix.shape[1]
        qkv_cols = q_cols + 2 * k_cols
        hidden_cols = gate_weight.shape[1] // 2
        me, mine = lax.axis_index("dp"), lax.axis_index("mp")

        def table(natural):
            entries = []
            for p in range(n):
                entry = jnp.int32(0)
                for axis, bit in enumerate(main_order):
                    digit, weight = ((p // bit) % 2, 1 << axis) if natural else ((p >> axis) % 2, bit)
                    if bit in others:
                        digit = ((me // bit) % 2 + digit) % 2
                    entry = entry + digit * weight
                entries.append(entry)
            return jnp.stack(entries)

        to_table, from_table = table(False), table(True)

        def own_first(array):
            return jnp.where(mine == 0, array, jnp.flip(array, 0))

        window = []

        def close(*results):
            window[:] = results

        def go(array):
            return after(array, *window) if window else array

        def gather_z(first, second):
            return along_z(go(jnp.concatenate([first, second, first, second], axis=0)))

        def gather_y(array):
            pieces = [array]
            for bit in others[:-1]:
                pieces = pieces + [swap(go(piece), bit) for piece in pieces]
            return pieces

        def gather_core(pieces):
            pieces = pieces + [swap(go(piece), 1) for piece in pieces]
            share = len(pieces) // PIECES
            if share > 1:
                pieces = [
                    jnp.concatenate(pieces[i * share : (i + 1) * share]) for i in range(PIECES)
                ]
            return pieces

        def halves(shard):
            return jnp.split(shard, 2, axis=1)

        def stage_columns(left, right, part, columns):
            first, count = part or (0, right.shape[1])
            columns = columns or (count if count < 1024 else 512)
            grid = (count // columns,)
            right = by_columns(right, columns, first // columns)
            return left.shape[0], count, columns, grid, right

        def stage_outs(height, count, columns, of):
            first, total, into = of or (0, count, ())
            out = ((height, total), BF16, (height, columns), lambda j: (0, j + first // columns))
            return out, into

        def for_core(left, right, part=None, of=None, columns=None):
            depth, count, columns, grid, right = stage_columns(left, go(right), part, columns)
            height = width // 2
            out, into = stage_outs(height, count, columns, of)
            return kernel_call(
                send_kernel,
                grid,
                [(left, (depth, height), lambda j: (0, 1)), right],
                [out],
                time=count / 240,
                into=into,
            )[0]

        def keep_core(left, right, other, part=None, of=None, columns=None, arrived=None):
            depth, count, columns, grid, right = stage_columns(left, go(right), part, columns)
            height = width // 2
            out, into = stage_outs(height // 2, count, columns, of)
            arrived = (part or (0, 0))[0] if arrived is None else arrived
            return kernel_call(
                keep_kernel,
                grid,
                [
                    (left, (depth, height), lambda j: (0, 0)),
                    right,
                    by_columns(other, columns, arrived // columns),
                ],
                [out] * 2,
                time=count / 240,
                into=into,
            )

        def swap_y(send):
            return swap(send, others[-2])

        def add_halves(keeps, others_sent):
            parts = [add_low(*pair_of) for pair_of in zip(keeps, others_sent)]
            return reduce_rest(jnp.concatenate(parts, axis=1))

        def reduce_rest(array):
            for bit in others[-3::-1]:
                half = array.shape[0] // 2
                array = add_low(array[:half], swap(array[half:], bit))
            return array

        def scatter_z(array):
            return along_z(go(array))

        def scatter_gains(gradients, *earlier):
            array = gradients.reshape(2, n, block).transpose(1, 0, 2)
            for bit in others[::-1]:
                half = array.shape[0] // 2
                array = array[:half] + swap(array[half:], bit)
            array = after(array, *earlier)
            for bit in (2 * pair, pair):
                array = array.reshape(2, -1, 2, block)
                digit = (me // bit) % 2
                keep = lax.dynamic_index_in_dim(array, digit, 0, False)
                array = keep + swap(lax.dynamic_index_in_dim(array, 1 - digit, 0, False), bit)
            return array[0]

        def gather_square_one(own):
            own = go(own)
            return own, swap_mp(own), swap(own, pair)

        def gather_square_two(own, by_mp, by_pair):
            return own, by_mp, by_pair, swap_mp(go(by_pair))

        def scatter_square_one(parts):
            mp_one, pair_one, mp_two, pair_two = parts
            return swap_mp(go(mp_one)), swap(go(pair_one), pair), mp_two, pair_two

        def scatter_square_two(mp_one, pair_one, mp_two, pair_two):
            mp_two = swap_mp(go(add_low(mp_two, pair_one[middle:])))
            pair_two = swap(go(add_low(pair_two, mp_one[middle:])), pair)
            return mp_one, pair_one, mp_two, pair_two

        def square_operands(own, mp_one, pair_one, mp_two, pair_two):
            top = lambda i: (0, 0)
            shape = (middle, width)
            return [
                by_rows(own, middle),
                (pair_one, shape, top),
                (mp_two, shape, top),
                (mp_one, shape, top),
                (pair_two, shape, top),
            ]

        def norm_back(gain_row, values, passed, sums):
            return kernel_call(
                functools.partial(norm_back_kernel, gain_row),
                (2,),
                [
                    by_rows(values, middle),
                    by_rows(passed, middle),
                    *square_operands(*sums),
                    whole(gains),
                ],
                [
                    ((rows, width), F32, (middle, width), lambda i: (i, 0)),
                    ((rows, width), BF16, (middle, width), lambda i: (i, 0)),
                    ((8, width), F32, (8, width), lambda i: (0, 0)),
                ],
                time=5,
            )

        own_rows = lambda i: (i, 0)
        shape = (1, rows, width)

        gain_cols = jnp.pad(jnp.stack([attn_gain, mlp_gain], axis=1), ((0, 0), (0, 126)))
        cut = q_cols - 128
        last_cols = qkv_cols - cut
        first_shard = query_weight[:, :cut]
        last_shard = jnp.concatenate(
            [query_weight[:, cut:], key_matrix, value_matrix, gain_cols], axis=1
        )
        first_z = gather_z(first_shard, first_shard)
        out_shard, down_shard = transposed(out_weight), transposed(down_weight)
        cot_own = lax.dynamic_index_in_dim(cotangent, mine, 0, True)
        close(first_z, cot_own)

        first_y = gather_y(first_z)
        last_z = gather_z(last_shard, last_shard)
        starts = own_first(seq_starts)
        positions = me * rows + jnp.arange(rows, dtype=jnp.int32)[None] - starts
        tables = rope_tables(positions.reshape(tokens))
        about = [by_rows(t, rows) for t in tables]
        about += [by_rows(starts[:, :, None], 1), by_rows(starts[:, None, :], 1)]
        close(*first_y, last_z, *tables, down_shard)

        last_y = gather_y(last_z)
        first_parts = gather_core(first_y)
        out_z = gather_z(out_shard, out_shard)
        close(*last_y, *first_parts)

        last_parts = gather_core(last_y)
        close(*last_parts, out_z)

        out_y = gather_y(out_z)
        gate_z = gather_z(*halves(gate_weight))
        moved = block % 128 == 0
        all_rows, turn = inputs, mine
        if not moved:
            all_rows, turn = move_blocks(inputs, to_table, mine, BF16), jnp.int32(0)
        rows_in, first_hidden, qkv_rot, attended, gains = kernel_call(
            functools.partial(attend_kernel, n if moved else 0, q_cols, k_cols),
            (2,),
            [
                (all_rows, shape, lambda i, t: ((i + t[n]) % 2, 0, 0)),
                *[whole(p) for p in first_parts],
                *[whole(p) for p in last_parts],
                *about,
            ],
            [
                ((tokens, width), BF16, (rows, width), lambda i, t: (i, 0)),
                ((tokens, width), BF16, (rows, width), lambda i, t: (i, 0)),
                ((tokens, qkv_cols), BF16, (rows, qkv_cols), lambda i, t: (i, 0)),
                ((tokens, q_cols), BF16, (rows, q_cols), lambda i, t: (i, 0)),
                ((8, width), F32, (8, width), lambda i, t: (0, 0)),
            ],
            scalars=(jnp.concatenate([to_table, turn[None]]),),
            scratch=[pltpu.VMEM((rows, qkv_cols), F32)],
            time=15,
        )
        close(attended, *out_y)

        out_parts = gather_core(out_y)
        branch_own, branch_other = times_back([(attended, out_parts)], rows)
        close(branch_other)

        branch_other = swap_mp(go(branch_other))
        close(gate_z, branch_other)
        gate_y = gather_y(gate_z)
        up_z = gather_z(*halves(up_weight))
        after_own, hidden_own = kernel_call(
            forward_norm_kernel,
            (2,),
            [
                by_rows(rows_in, middle),
                by_rows(branch_own, middle),
                by_rows(branch_other, middle),
                whole(gains),
            ],
            [
                ((rows, width), F32, (middle, width), own_rows),
                ((rows, width), BF16, (middle, width), own_rows),
            ],
        )
        close(hidden_own)

        hidden_parts = gather_square_one(hidden_own)
        close(*hidden_parts, *gate_y, up_z)

        hidden_parts = gather_square_two(*hidden_parts)
        gate_parts = gather_core(gate_y)
        up_y = gather_y(up_z)
        down_quarters = jnp.split(down_shard, 4, axis=1)
        down_one_z = gather_z(*down_quarters[::2])
        cot_pair = swap(go(cot_own), pair)
        close(*hidden_parts, *gate_parts)

        columns = 512
        grid = (hidden_cols // columns,)
        half_hidden = hidden_cols // 2
        column_halves = ((0, half_hidden), (half_hidden, half_hidden))
        hidden_out = ((pair_tokens, hidden_cols), BF16, (pair_tokens, columns), lambda j: (0, j))
        hidden_two, gate_val = kernel_call(
            gate_kernel,
            grid,
            [
                *[whole(a) for a in hidden_parts],
                *[by_columns(p, columns) for p in gate_parts],
            ],
            [
                ((pair_tokens, width), BF16, (pair_tokens, width), lambda j: (0, 0)),
                hidden_out,
            ],
            time=14,
        )
        close(*up_y, gate_val)

        up_parts = gather_core(up_y)
        cot_both = swap_mp(go(cot_pair))
        down_two_z = gather_z(*down_quarters[1::2])
        down_one_y = gather_y(down_one_z)
        close(*up_parts)
        up_val, mixed = kernel_call(
            up_kernel,
            grid,
            [
                whole(hidden_two),
                *[by_columns(p, columns) for p in up_parts],
                by_columns(gate_val, columns),
            ],
            [hidden_out, hidden_out],
            time=16,
        )
        cot_all = jnp.zeros((4, rows, width), BF16)
        cot_all = move_blocks(cotangent, to_table, mine, BF16, cot_all)
        none = jnp.int32(0)
        cot_all = move_blocks(cot_pair, to_table, none, BF16, cot_all, 2)
        cot_all = move_blocks(after(cot_both, mixed), to_table, none, BF16, cot_all, 3)
        cot_all = cot_all.reshape(pair_tokens, width)
        close(mixed, *down_one_y, down_two_z, cot_all)

        down_two_y = gather_y(down_two_z)
        down_one = gather_core(down_one_y)
        close(*down_one)

        def mixed_back(parts, first, into=()):
            place = lambda j: (0, j + first)
            out = ((pair_tokens, hidden_cols), BF16, (pair_tokens, columns), place)
            return kernel_call(
                mixed_back_kernel,
                (hidden_cols // columns // 2,),
                [
                    whole(cot_all),
                    *[by_columns(p, columns) for p in parts],
                    by_columns(gate_val, columns, first),
                    by_columns(go(up_val), columns, first),
                ],
                [out, out],
                time=9,
                into=into,
            )

        acts = mixed_back(down_one, 0)
        down_sent = for_core(cot_all, after(mixed, acts[0]))
        close(down_sent, *down_two_y)

        down_two = gather_core(down_two_y)
        down_sent = swap(go(down_sent), 1)
        close(*down_two, down_sent)
        down_keep, down_send = keep_core(cot_all, mixed, down_sent)
        close(down_keep)
        down_arrived = swap_y(go(down_send))
        grad_gate_act, grad_up_act = mixed_back(down_two, hidden_cols // columns // 2, acts)
        sides = [(grad_gate_act, gate_parts), (grad_up_act, up_parts)]
        grad_two_own, *grad_two = times_back(sides, rows)
        close(grad_two_own)

        grad_two = scatter_square_one(grad_two)
        gate_sent = for_core(hidden_two, grad_gate_act)
        up_sent = for_core(hidden_two, after(grad_up_act, gate_sent))
        grad_down = reduce_rest(add_low(go(down_keep), down_arrived))
        close(*grad_two[:2], gate_sent, up_sent, grad_down)

        grad_two = scatter_square_two(*grad_two)
        gate_sent, up_sent = swap(go(gate_sent), 1), swap(go(up_sent), 1)
        low, high = column_halves
        gate_low = keep_core(hidden_two, grad_gate_act, gate_sent, low)
        close(*grad_two)
        grad_down = scatter_z(go(grad_down))
        close(*grad_two, *gate_low)
        gate_first = swap_y(go(gate_low[1]))
        grad_after, grad_branch, gain_two = norm_back(
            1, after_own, cot_all, (grad_two_own, *grad_two)
        )
        close(grad_branch)

        branch_other = swap_mp(go(grad_branch))
        gate_high = keep_core(hidden_two, grad_gate_act, gate_sent, high)
        gate_second = swap_y(gate_high[1])

        def attention_back(branch, which, into=()):
            block_at = lambda i: (which, 0)
            return kernel_call(
                functools.partial(attend_back_kernel, q_cols, k_cols),
                (1,),
                [
                    whole(branch),
                    *[whole(p) for p in (*out_parts, *first_parts, *last_parts)],
                    (go(qkv_rot), (rows, qkv_cols), block_at),
                    *[
                        (array, part, lambda i, d=array.ndim: (which,) + (0,) * (d - 1))
                        for array, part, _ in about
                    ],
                ],
                [
                    ((tokens, width), BF16, (rows, width), block_at),
                    ((tokens, qkv_cols), BF16, (rows, qkv_cols), block_at),
                    ((rows, width), BF16, (rows, width), lambda i: (0, 0)),
                ],
                scratch=[pltpu.VMEM((rows, q_cols), BF16)],
                time=15,
                into=into,
            )

        *backs, one_own = attention_back(grad_branch, 0)
        up_low = keep_core(hidden_two, after(grad_up_act, one_own), up_sent, low)
        close(branch_other, *up_low, one_own, grad_down, gate_first, gate_second)

        up_first = swap_y(go(up_low[1]))
        grad_gate = scatter_z(add_halves((gate_low[0], gate_high[0]), (gate_first, gate_second)))
        one_from_other = swap_mp(go(one_own))
        grad_branch, grad_qkv, one_other = attention_back(branch_other, 1, backs)
        up_high = keep_core(hidden_two, after(grad_up_act, one_other), up_sent, high)
        up_keep, up_send = zip(up_low, up_high)
        close(one_other, up_first, up_high[1], one_from_other)

        one_from_own = swap_mp(go(one_other))
        up_second = swap_y(go(up_send[1]))
        total = q_cols + qkv_cols
        sent = for_core(grad_branch, attended, of=(0, total, ()))
        sent = for_core(first_hidden, grad_qkv, of=(q_cols, total, (sent,)))
        sides = [(go(mixed), down_one), (mixed, down_two, 1)]
        branch_two_own, *branch_two = times_back(sides, rows)
        close(sent, up_second, grad_gate, branch_two_own, one_from_own)

        sent = swap(go(sent), 1)
        grad_up = scatter_z(add_halves(up_keep, (up_first, up_second)))
        branch_two = scatter_square_one(branch_two)
        close(sent)
        half, rest = total // 2, total // 2 - q_cols
        group_one = keep_core(grad_branch, attended, sent, None, (0, half, ()), 256)
        group_one = keep_core(
            first_hidden, grad_qkv, sent, (0, rest), (q_cols, half, group_one), 256, q_cols
        )
        group_two = keep_core(
            first_hidden, grad_qkv, sent, (rest, half), (0, half, ()), 256, half
        )
        close(*group_one, *group_two)

        y_one = swap_y(go(group_one[1]))
        y_two = swap_y(after(group_two[1], y_one))
        latest = lambda i, *_: (jnp.minimum(i, 1), 0)
        later = lambda i, *_: (jnp.maximum(i - 2, 0), 0)
        half_rows = (middle, width)
        input_grad, gain_one = kernel_call(
            functools.partial(last_norm_back_kernel, n if moved else 0),
            (4,),
            [
                by_rows(rows_in, middle),
                by_rows(grad_branch, middle),
                (one_own, half_rows, latest),
                (one_other, half_rows, later),
                (one_from_own, half_rows, latest),
                (one_from_other, half_rows, later),
                whole(gains),
            ],
            [
                (
                    (micro_count, rows, width),
                    F32,
                    (1, middle, width),
                    lambda i, t: ((i // 2 + t[n]) % 2, i % 2, 0),
                ),
                ((8, width), F32, (8, width), lambda i, t: (0, 0)),
            ],
            scalars=(jnp.concatenate([from_table, turn[None]]),),
            scratch=[pltpu.VMEM((1, middle, width), F32)],
            time=5,
        )
        if not moved:
            input_grad = move_blocks(input_grad, from_table, mine, F32)
        grad_down = owned(go(grad_down), None, block, True, True)
        grad_gate = owned(go(grad_gate), None, block, True, False)
        sum_one = reduce_rest(add_low(after(group_one[0], gain_one, grad_down, grad_gate), y_one))
        z_one = along_z(after(sum_one, grad_up))
        z_two = along_z(after(reduce_rest(add_low(group_two[0], y_two)), z_one))
        close(y_one, *branch_two[:2])
        branch_two = scatter_square_two(*branch_two)
        result = kernel_call(
            add_kernel,
            (2,),
            [
                by_rows(after_own, middle),
                *square_operands(branch_two_own, *branch_two),
            ],
            [((rows, width), BF16, (middle, width), own_rows)],
        )[0]
        other_result = swap_mp(result)
        gain_two = gain_two[0] + swap_mp(gain_two[0])
        grad_up = owned(after(grad_up, result), None, block, True, False)
        grad_gains = scatter_gains(jnp.stack([gain_one[0], gain_two]), grad_up)
        output = move_blocks(jnp.stack([result, other_result]), from_table, mine, BF16)
        grad_out, *grad_attn = owned_columns(
            after(z_one, grad_up), z_two, block, (q_cols, rest, k_cols)
        )
        return (
            output,
            input_grad,
            grad_gains[0],
            *grad_attn,
            grad_out,
            grad_gains[1],
            grad_gate,
            grad_up,
            grad_down,
        )

    return per_device


def solution(mesh):
    in_specs = (
        P(None, "dp", None),
        P(None, "dp"),
        P(None, "dp", None),
        P("dp"),
        P("dp", "mp"),
        P("dp", "mp"),
        P("dp", "mp"),
        P("mp", "dp"),
        P("dp"),
        P("dp", "mp"),
        P("dp", "mp"),
        P("mp", "dp"),
    )
    out_specs = (
        P(None, "dp", None),
        P(None, "dp", None),
        P("dp"),
        P("dp", "mp"),
        P("dp", "mp"),
        P("dp", "mp"),
        P("mp", "dp"),
        P("dp"),
        P("dp", "mp"),
        P("dp", "mp"),
        P("mp", "dp"),
    )
    return jax.shard_map(
        make_per_device(mesh.shape["dp"]),
        mesh=mesh,
        in_specs=in_specs,
        out_specs=out_specs,
        check_vma=False,
    )
```

profile of v0, /device:TPU:0, one launch (start us, length us, event | category | flops | bytes accessed | tf_op | source)
XLA Modules:
  0.0 690.2 jit_solution(16681837860090971462)
XLA Ops:
  2.8 6.4 all-to-all-start
  10.5 5.1 maximum_maximum_fusion
  15.6 16.6 %all-to-all-done = bf16[4,128,896]{2,1,0:T(8,128)(2,1)S(1)} async-done(((bf16[4,128,896]{2,1,0:T(8,128)(2,1)}), bf16[4,128,896]{2,1,0:T(8,128)(2,1)S(1)}, u32[]{:S(2)}, u32[]{:S(2)}) %all-to-all-start) | async-done | bytes 917536 | tf_op jit(solution)/shard_map/all_to_all | solution.py:579
  37.4 5.5 shard_map.203
  46.6 10.7 %collective-permute-done.refs_1_.refs_5_ = bf16[512,896]{1,0:T(8,128)(2,1)} collective-permute-done((bf16[512,896]{1,0:T(8,128)(2,1)S(1)}, bf16[512,896]{1,0:T(8,128)(2,1)}, u32[]{:S(2)}, u32[]{:S(2)}) %collective-permute-start) | collective-permute-done | bytes 917536 | tf_op jit(solution)/shard_map/ppermute | solution.py:573
  61.7 4.7 all-to-all-start.2
  66.4 11.1 %collective-permute-done.3.refs_5_.refs_9_ = bf16[512,768]{1,0:T(8,128)(2,1)} collective-permute-done((bf16[512,768]{1,0:T(8,128)(2,1)S(1)}, bf16[512,768]{1,0:T(8,128)(2,1)}, u32[]{:S(2)}, u32[]{:S(2)}) %collective-permute-start.3) | collective-permute-done | bytes 786464 | tf_op jit(solution)/shard_map/ppermute | solution.py:573
  80.3 11.8 %all-to-all-done.2 = bf16[4,128,1024]{2,1,0:T(8,128)(2,1)S(1)} async-done(((bf16[4,128,1024]{2,1,0:T(8,128)(2,1)}), bf16[4,128,1024]{2,1,0:T(8,128)(2,1)S(1)}, u32[]{:S(2)}, u32[]{:S(2)}) %all-to-all-start.2) | async-done | bytes 1048608 | tf_op jit(solution)/shard_map/all_to_all | solution.py:579
  102.2 14.8 %shard_map.204 = (bf16[512,2048]{1,0:T(8,128)(2,1)}, bf16[512,2048]{1,0:T(8,128)(2,1)}, bf16[512,1536]{1,0:T(8,128)(2,1)}, bf16[512,1024]{1,0:T(8,128)(2,1)}, f32[8,2048]{1,0:T(8,128)}) custom-call(s32[17]{0:T(128)} %concatenate.50.table_ref, bf16[2,256,2048]{2,1,0:T(8,128)(2,1)} %in_ref.5, bf16[512,896]{1,0:T(8,128)(2,1)} %bitcast.103, ...), custom_call_target="tpu_custom_call" | custom-call | flops 1 | bytes 15000 | tf_op jit(solution)/shard_map/pallas_call | solution.py:47
  122.4 6.4 shard_map.206
  131.9 22.3 %collective-permute-done.9.other_ref = bf16[256,2048]{1,0:T(8,128)(2,1)} collective-permute-done((bf16[256,2048]{1,0:T(8,128)(2,1)}, bf16[256,2048]{1,0:T(8,128)(2,1)}, u32[]{:S(2)}, u32[]{:S(2)}) %collective-permute-start.9) | collective-permute-done | bytes 1048608 | tf_op jit(solution)/shard_map/ppermute | solution.py:576
  154.3 5.1 all-to-all-start.4
  168.1 20.6 %collective-permute-done.10.refs_1_ = bf16[256,2048]{1,0:T(8,128)(2,1)} collective-permute-done((bf16[256,2048]{1,0:T(8,128)(2,1)}, bf16[256,2048]{1,0:T(8,128)(2,1)}, u32[]{:S(2)}, u32[]{:S(2)}) %collective-permute-start.10) | collective-permute-done | bytes 1048608 | tf_op jit(solution)/shard_map/ppermute | solution.py:576
  188.7 28.8 %collective-permute-done.11.refs_2_ = bf16[256,2048]{1,0:T(8,128)(2,1)} collective-permute-done((bf16[256,2048]{1,0:T(8,128)(2,1)}, bf16[256,2048]{1,0:T(8,128)(2,1)}, u32[]{:S(2)}, u32[]{:S(2)}) %collective-permute-start.11) | collective-permute-done | bytes 1048608 | tf_op jit(solution)/shard_map/ppermute | solution.py:573
  228.7 16.8 %collective-permute-done.13.refs_3_ = bf16[256,2048]{1,0:T(8,128)(2,1)} collective-permute-done((bf16[256,2048]{1,0:T(8,128)(2,1)}, bf16[256,2048]{1,0:T(8,128)(2,1)}, u32[]{:S(2)}, u32[]{:S(2)}) %collective-permute-start.13) | collective-permute-done | bytes 1048608 | tf_op jit(solution)/shard_map/ppermute | solution.py:576
  245.6 13.8 %shard_map.208 = (bf16[1024,2048]{1,0:T(8,128)(2,1)}, bf16[1024,2048]{1,0:T(8,128)(2,1)}) custom-call(bf16[256,2048]{1,0:T(8,128)(2,1)} %get-tuple-element.171.refs_0_, bf16[256,2048]{1,0:T(8,128)(2,1)} %collective-permute-done.10.refs_1_, bf16[256,2048]{1,0:T(8,128)(2,1)} %collective-permute-done.11.refs_2_, ...), custom_call_target="tpu_custom_call" | custom-call | flops 1 | bytes 14000 | tf_op jit(solution)/shard_map/pallas_call | solution.py:47
  259.3 6.6 collective-permute-done.16.refs_1_.refs_7_
  284.5 15.3 %shard_map.209 = (bf16[1024,2048]{1,0:T(8,128)(2,1)}, bf16[1024,2048]{1,0:T(8,128)(2,1)}) custom-call(bf16[1024,2048]{1,0:T(8,128)(2,1)} %get-tuple-element.178.all_ref.left_ref, bf16[512,2048]{1,0:T(8,128)(2,1)} %bitcast.45.refs_0_.refs_6_, bf16[512,2048]{1,0:T(8,128)(2,1)} %collective-permute-done.16.refs_1_.refs_7_, ...), custom_call_target="tpu_custom_call" | custom-call | flops 1 | bytes 16000 | tf_op jit(solution)/shard_map/pallas_call | solution.py:47
  308.3 11.1 %shard_map.213 = (bf16[1024,2048]{1,0:T(8,128)(2,1)}, bf16[1024,2048]{1,0:T(8,128)(2,1)}) custom-call(bf16[1024,2048]{1,0:T(8,128)(2,1)} %bitcast.87, bf16[512,1024]{1,0:T(8,128)(2,1)} %bitcast.113, bf16[512,1024]{1,0:T(8,128)(2,1)} %copy-done.16, bf16[512,1024]{1,0:T(8,128)(2,1)} %copy-done.17, bf16[512,1024]{1,0:T(8,128)(2,1)} %copy-done.18, ...), custom_call_target="tpu_custom_call" | custom-call | flops 1 | bytes 9000 | tf_op jit(solution)/shard_map/pallas_call | solution.py:47
  319.3 8.6 %shard_map.214 = bf16[1024,2048]{1,0:T(8,128)(2,1)} custom-call(bf16[1024,2048]{1,0:T(8,128)(2,1)} %bitcast.88, bf16[1024,2048]{1,0:T(8,128)(2,1)} %get-tuple-element.250.right_ref.refs_0_.refs_1_), custom_call_target="tpu_custom_call" | custom-call | flops 1 | bytes 8533 | tf_op jit(solution)/shard_map/pallas_call | solution.py:47
  329.4 8.4 %collective-permute-done.25.refs_2_.refs_8_ = bf16[512,1024]{1,0:T(8,128)(2,1)S(1)} collective-permute-done((bf16[512,1024]{1,0:T(8,128)(2,1)S(1)}, bf16[512,1024]{1,0:T(8,128)(2,1)S(1)}, u32[]{:S(2)}, u32[]{:S(2)}) %collective-permute-start.25) | collective-permute-done | bytes 1048608 | tf_op jit(solution)/shard_map/ppermute | solution.py:573
  341.3 9.0 %shard_map.215 = (bf16[512,2048]{1,0:T(8,128)(2,1)}, bf16[512,2048]{1,0:T(8,128)(2,1)}) custom-call(bf16[1024,2048]{1,0:T(8,128)(2,1)} %bitcast.89, bf16[1024,2048]{1,0:T(8,128)(2,1)} %get-tuple-element.250.right_ref.refs_0_.refs_1_, bf16[1024,2048]{1,0:T(8,128)(2,1)} %copy-done.15), custom_call_target="tpu_custom_call" | custom-call | flops 1 | bytes 8533 | tf_op jit(solution)/shard_map/pallas_call | solution.py:47
  350.8 11.1 %shard_map.216 = (bf16[1024,2048]{1,0:T(8,128)(2,1)}, bf16[1024,2048]{1,0:T(8,128)(2,1)}) custom-call(bf16[1024,2048]{1,0:T(8,128)(2,1)} %bitcast.90, bf16[512,1024]{1,0:T(8,128)(2,1)} %bitcast.117, bf16[512,1024]{1,0:T(8,128)(2,1)} %collective-permute-done.22.refs_1_.refs_7_, ...), custom_call_target="tpu_custom_call", output_to_operand_aliasing={{0}: (7, {}), {1}: (8, {})} | custom-call | flops 1 | bytes 9000 | tf_op jit(solution)/shard_map/pallas_call | solution.py:47
  361.9 28.2 %shard_map.217 = (bf16[256,2048]{1,0:T(8,128)(2,1)}, bf16[256,2048]{1,0:T(8,128)(2,1)}, bf16[256,2048]{1,0:T(8,128)(2,1)}, bf16[128,2048]{1,0:T(8,128)(2,1)}, bf16[128,2048]{1,0:T(8,128)(2,1)}) custom-call(bf16[1024,2048]{1,0:T(8,128)(2,1)} %get-tuple-element.239.refs_0_.right_ref, bf16[1024,2048]{1,0:T(8,128)(2,1)} %get-tuple-element.247.refs_1_.right_ref, ...), custom_call_target="tpu_custom_call" | custom-call | flops 1 | bytes 28000 | tf_op jit(solution)/shard_map/pallas_call | solution.py:47
  392.7 8.5 %shard_map.218 = bf16[1024,2048]{1,0:T(8,128)(2,1)} custom-call(bf16[1024,2048]{1,0:T(8,128)(2,1)} %get-tuple-element.178.all_ref.left_ref, bf16[1024,2048]{1,0:T(8,128)(2,1)} %get-tuple-element.239.refs_0_.right_ref), custom_call_target="tpu_custom_call" | custom-call | flops 1 | bytes 8533 | tf_op jit(solution)/shard_map/pallas_call | solution.py:47
  401.2 8.7 %shard_map.219 = bf16[1024,2048]{1,0:T(8,128)(2,1)} custom-call(bf16[1024,2048]{1,0:T(8,128)(2,1)} %get-tuple-element.178.all_ref.left_ref, bf16[1024,2048]{1,0:T(8,128)(2,1)} %get-tuple-element.247.refs_1_.right_ref), custom_call_target="tpu_custom_call" | custom-call | flops 1 | bytes 8533 | tf_op jit(solution)/shard_map/pallas_call | solution.py:47
  419.1 12.7 %collective-permute-done.31.refs_2_ = bf16[128,2048]{1,0:T(8,128)(2,1)} collective-permute-done((bf16[128,2048]{1,0:T(8,128)(2,1)S(1)}, bf16[128,2048]{1,0:T(8,128)(2,1)}, u32[]{:S(2)}, u32[]{:S(2)}) %collective-permute-start.31) | collective-permute-done | bytes 524320 | tf_op jit(solution)/shard_map/ppermute | solution.py:576
  435.7 5.8 shard_map.223
  443.0 5.5 shard_map.220
  448.6 6.0 shard_map.224
  456.5 17.8 %shard_map.221 = (bf16[512,2048]{1,0:T(8,128)(2,1)}, bf16[512,1536]{1,0:T(8,128)(2,1)}, bf16[256,2048]{1,0:T(8,128)(2,1)}) custom-call(bf16[256,2048]{1,0:T(8,128)(2,1)} %get-tuple-element.223.branch_ref, bf16[512,1024]{1,0:T(8,128)(2,1)} %bitcast.99, bf16[512,1024]{1,0:T(8,128)(2,1)} %collective-permute-done.6.refs_2_.refs_1_, bf16[512,1024]{1,0:T(8,128)(2,1)} %copy-done.6, ...), custom_call_target="tpu_custom_call" | custom-call | flops 1 | bytes 15000 | tf_op jit(solution)/shard_map/pallas_call | solution.py:47
  474.4 5.9 shard_map.222
  480.7 7.1 %collective-permute-done.37 = bf16[512,1024]{1,0:T(8,128)(2,1)S(1)} collective-permute-done((bf16[512,1024]{1,0:T(8,128)(2,1)}, bf16[512,1024]{1,0:T(8,128)(2,1)S(1)}, u32[]{:S(2)}, u32[]{:S(2)}) %collective-permute-start.37) | collective-permute-done | bytes 1048608 | tf_op jit(solution)/shard_map/ppermute | solution.py:573
  490.9 4.8 all-to-all-start.8
  498.7 17.8 %shard_map.225 = (bf16[512,2048]{1,0:T(8,128)(2,1)}, bf16[512,1536]{1,0:T(8,128)(2,1)}, bf16[256,2048]{1,0:T(8,128)(2,1)}) custom-call(bf16[256,2048]{1,0:T(8,128)(2,1)} %collective-permute-done.33.branch_ref, bf16[512,1024]{1,0:T(8,128)(2,1)} %bitcast.100, ...), custom_call_target="tpu_custom_call", output_to_operand_aliasing={{0}: (18, {}), {1}: (19, {})} | custom-call | flops 1 | bytes 15000 | tf_op jit(solution)/shard_map/pallas_call | solution.py:47
  516.5 5.9 shard_map.226
  527.4 5.7 shard_map.229
  533.2 15.3 %shard_map.227 = (bf16[256,2048]{1,0:T(8,128)(2,1)}, bf16[256,2048]{1,0:T(8,128)(2,1)}, bf16[256,2048]{1,0:T(8,128)(2,1)}, bf16[128,2048]{1,0:T(8,128)(2,1)}, bf16[128,2048]{1,0:T(8,128)(2,1)}) custom-call(bf16[1024,2048]{1,0:T(8,128)(2,1)} %get-tuple-element.250.right_ref.refs_0_.refs_1_, bf16[1024,2048]{1,0:T(8,128)(2,1)} %get-tuple-element.250.right_ref.refs_0_.refs_1_, ...), custom_call_target="tpu_custom_call" | custom-call | flops 1 | bytes 28000 | tf_op jit(solution)/shard_map/pallas_call | solution.py:47
  552.9 5.3 all-to-all-start.9
  558.2 5.2 shard_map.230
  563.3 6.2 shard_map.232
  576.5 8.8 %shard_map.235 = (f32[2,256,2048]{2,1,0:T(8,128)}, f32[8,2048]{1,0:T(8,128)}) custom-call(s32[17]{0:T(128)} %concatenate.49.table_ref, bf16[512,2048]{1,0:T(8,128)(2,1)} %get-tuple-element.161.rows_ref.values_ref, bf16[512,2048]{1,0:T(8,128)(2,1)} %get-tuple-element.256.left_ref.passed_ref, bf16[256,2048]{1,0:T(8,128)(2,1)} %get-tuple-element.249.refs_0_, ...), custom_call_target="tpu_custom_call" | custom-call | flops 1 | bytes 5000 | tf_op jit(solution)/shard_map/pallas_call | solution.py:47
  593.5 9.2 %collective-permute-done.44 = bf16[512,1280]{1,0:T(8,128)(2,1)S(1)} collective-permute-done((bf16[512,1280]{1,0:T(8,128)(2,1)}, bf16[512,1280]{1,0:T(8,128)(2,1)S(1)}, u32[]{:S(2)}, u32[]{:S(2)}) %collective-permute-start.44) | collective-permute-done | bytes 1310752 | tf_op jit(solution)/shard_map/ppermute | solution.py:573
  613.9 6.6 collective-permute-done.42.pair_one
  626.2 13.8 %collective-permute-done.54 = bf16[512,1280]{1,0:T(8,128)(2,1)S(1)} collective-permute-done((bf16[512,1280]{1,0:T(8,128)(2,1)}, bf16[512,1280]{1,0:T(8,128)(2,1)S(1)}, u32[]{:S(2)}, u32[]{:S(2)}) %collective-permute-start.54) | collective-permute-done | bytes 1310752 | tf_op jit(solution)/shard_map/ppermute | solution.py:573
  641.4 4.7 all-to-all-start.11
  647.0 4.5 collective-permute-done.47.pair_two
  665.0 10.6 %collective-permute-done.52 = f32[2,2,128]{2,1,0:T(2,128)S(1)} collective-permute-done((f32[2,2,128]{2,1,0:T(2,128)S(1)}, f32[2,2,128]{2,1,0:T(2,128)S(1)}, u32[]{:S(2)}, u32[]{:S(2)}) %collective-permute-start.52) | collective-permute-done | bytes 2080 | tf_op jit(solution)/shard_map/ppermute | solution.py:573
  (270 shorter events, 187.9 us)
Async XLA Ops:
  2.8 29.4 %all-to-all-start = ((bf16[4,128,896]{2,1,0:T(8,128)(2,1)}), bf16[4,128,896]{2,1,0:T(8,128)(2,1)S(1)}, u32[]{:S(2)}, u32[]{:S(2)}) async-start(bf16[4,128,896]{2,1,0:T(8,128)(2,1)} %bitcast.128), calls=%async_computation | async-start | bytes 1835008 | tf_op jit(solution)/shard_map/all_to_all | solution.py:579
  32.2 25.1 %all-to-all-start.1 = ((bf16[4,128,768]{2,1,0:T(8,128)(2,1)}), bf16[4,128,768]{2,1,0:T(8,128)(2,1)S(1)}, u32[]{:S(2)}, u32[]{:S(2)}) async-start(bf16[4,128,768]{2,1,0:T(8,128)(2,1)} %bitcast.37), calls=%async_computation.1 | async-start | bytes 1572864 | tf_op jit(solution)/shard_map/all_to_all | solution.py:579
  35.8 21.5 %collective-permute-start = (bf16[512,896]{1,0:T(8,128)(2,1)S(1)}, bf16[512,896]{1,0:T(8,128)(2,1)}, u32[]{:S(2)}, u32[]{:S(2)}) collective-permute-start(bf16[512,896]{1,0:T(8,128)(2,1)S(1)} %bitcast.101), channel_id=1, source_target_pairs={{0,4},{2,6},{4,0},{6,2},{8,12},{10,14},{12,8},{14,10},{16,20},{18,... | collective-permute-start | bytes 2752520 | tf_op jit(solution)/shard_map/ppermute | solution.py:573
  57.3 20.2 %collective-permute-start.1 = (bf16[512,896]{1,0:T(8,128)(2,1)S(1)}, bf16[512,896]{1,0:T(8,128)(2,1)}, u32[]{:S(2)}, u32[]{:S(2)}) collective-permute-start(bf16[512,896]{1,0:T(8,128)(2,1)S(1)} %bitcast.102), channel_id=1, source_target_pairs={{0,2},{2,0},{4,6},{6,4},{8,10},{10,8},{12,14},{14,12},{16,18},{18,... | collective-permute-start | bytes 2752520 | tf_op jit(solution)/shard_map/ppermute | solution.py:573
  57.4 20.1 %collective-permute-start.2 = (bf16[512,896]{1,0:T(8,128)(2,1)}, bf16[512,896]{1,0:T(8,128)(2,1)}, u32[]{:S(2)}, u32[]{:S(2)}) collective-permute-start(bf16[512,896]{1,0:T(8,128)(2,1)} %collective-permute-done.refs_1_.refs_5_), channel_id=1, source_target_pairs={{0,2},{2,0},{4,6},{6,4},{8,10},{10,8},{12,14},{14,12},{16,18},{18,... | collective-permute-start | bytes 2752520 | tf_op jit(solution)/shard_map/ppermute | solution.py:573
  57.9 19.6 %collective-permute-start.3 = (bf16[512,768]{1,0:T(8,128)(2,1)S(1)}, bf16[512,768]{1,0:T(8,128)(2,1)}, u32[]{:S(2)}, u32[]{:S(2)}) collective-permute-start(bf16[512,768]{1,0:T(8,128)(2,1)S(1)} %bitcast.106), channel_id=1, source_target_pairs={{0,4},{2,6},{4,0},{6,2},{8,12},{10,14},{12,8},{14,10},{16,20},{18,... | collective-permute-start | bytes 2359304 | tf_op jit(solution)/shard_map/ppermute | solution.py:573
  61.7 30.4 %all-to-all-start.2 = ((bf16[4,128,1024]{2,1,0:T(8,128)(2,1)}), bf16[4,128,1024]{2,1,0:T(8,128)(2,1)S(1)}, u32[]{:S(2)}, u32[]{:S(2)}) async-start(bf16[4,128,1024]{2,1,0:T(8,128)(2,1)} %bitcast.125), calls=%async_computation.2 | async-start | bytes 2097152 | tf_op jit(solution)/shard_map/all_to_all | solution.py:579
  92.1 24.8 %collective-permute-start.6 = (bf16[512,1024]{1,0:T(8,128)(2,1)S(1)}, bf16[512,1024]{1,0:T(8,128)(2,1)}, u32[]{:S(2)}, u32[]{:S(2)}) collective-permute-start(bf16[512,1024]{1,0:T(8,128)(2,1)S(1)} %bitcast.96), channel_id=1, source_target_pairs={{0,4},{2,6},{4,0},{6,2},{8,12},{10,14},{12,8},{14,10},{16,20},{18,... | collective-permute-start | bytes 3145736 | tf_op jit(solution)/shard_map/ppermute | solution.py:573
  95.8 58.5 %all-to-all-start.3 = ((bf16[4,128,2048]{2,1,0:T(8,128)(2,1)}), bf16[4,128,2048]{2,1,0:T(8,128)(2,1)S(1)}, u32[]{:S(2)}, u32[]{:S(2)}) async-start(bf16[4,128,2048]{2,1,0:T(8,128)(2,1)} %bitcast.119), calls=%async_computation.3 | async-start | bytes 4194304 | tf_op jit(solution)/shard_map/all_to_all | solution.py:579
  128.8 25.5 %collective-permute-start.9 = (bf16[256,2048]{1,0:T(8,128)(2,1)}, bf16[256,2048]{1,0:T(8,128)(2,1)}, u32[]{:S(2)}, u32[]{:S(2)}) collective-permute-start(bf16[256,2048]{1,0:T(8,128)(2,1)} %get-tuple-element.168), channel_id=1, source_target_pairs={{0,1},{1,0},{2,3},{3,2},{4,5},{5,4},{6,7},{7,6},{8,9},{9,8},{10,11... | collective-permute-start | bytes 3145736 | tf_op jit(solution)/shard_map/ppermute | solution.py:576
  154.3 63.2 %all-to-all-start.4 = ((bf16[4,128,2048]{2,1,0:T(8,128)(2,1)}), bf16[4,128,2048]{2,1,0:T(8,128)(2,1)}, u32[]{:S(2)}, u32[]{:S(2)}) async-start(bf16[4,128,2048]{2,1,0:T(8,128)(2,1)} %bitcast.122), calls=%async_computation.4 | async-start | bytes 4194304 | tf_op jit(solution)/shard_map/all_to_all | solution.py:579
  159.4 58.1 %collective-permute-start.12 = (bf16[512,2048]{1,0:T(8,128)(2,1)S(1)}, bf16[512,2048]{1,0:T(8,128)(2,1)}, u32[]{:S(2)}, u32[]{:S(2)}) collective-permute-start(bf16[512,2048]{1,0:T(8,128)(2,1)S(1)} %bitcast.92), channel_id=1, source_target_pairs={{0,4},{2,6},{4,0},{6,2},{8,12},{10,14},{12,8},{14,10},{16,20},{18,... | collective-permute-start | bytes 6291464 | tf_op jit(solution)/shard_map/ppermute | solution.py:573
  164.6 24.1 %collective-permute-start.10 = (bf16[256,2048]{1,0:T(8,128)(2,1)}, bf16[256,2048]{1,0:T(8,128)(2,1)}, u32[]{:S(2)}, u32[]{:S(2)}) collective-permute-start(bf16[256,2048]{1,0:T(8,128)(2,1)} %get-tuple-element.171.refs_0_), channel_id=1, source_target_pairs={{0,1},{1,0},{2,3},{3,2},{4,5},{5,4},{6,7},{7,6},{8,9},{9,8},{10,11... | collective-permute-start | bytes 3145736 | tf_op jit(solution)/shard_map/ppermute | solution.py:576
  166.1 51.4 %collective-permute-start.11 = (bf16[256,2048]{1,0:T(8,128)(2,1)}, bf16[256,2048]{1,0:T(8,128)(2,1)}, u32[]{:S(2)}, u32[]{:S(2)}) collective-permute-start(bf16[256,2048]{1,0:T(8,128)(2,1)} %get-tuple-element.171.refs_0_), channel_id=1, source_target_pairs={{0,8},{2,10},{4,12},{6,14},{8,0},{10,2},{12,4},{14,6},{16,24},{18,... | collective-permute-start | bytes 3145736 | tf_op jit(solution)/shard_map/ppermute | solution.py:573
  217.5 28.1 %collective-permute-start.14 = (bf16[512,2048]{1,0:T(8,128)(2,1)S(1)}, bf16[512,2048]{1,0:T(8,128)(2,1)}, u32[]{:S(2)}, u32[]{:S(2)}) collective-permute-start(bf16[512,2048]{1,0:T(8,128)(2,1)S(1)} %bitcast.93), channel_id=1, source_target_pairs={{0,2},{2,0},{4,6},{6,4},{8,10},{10,8},{12,14},{14,12},{16,18},{18,... | collective-permute-start | bytes 6291464 | tf_op jit(solution)/shard_map/ppermute | solution.py:573
  217.6 28.0 %collective-permute-start.15 = (bf16[512,2048]{1,0:T(8,128)(2,1)}, bf16[512,2048]{1,0:T(8,128)(2,1)}, u32[]{:S(2)}, u32[]{:S(2)}) collective-permute-start(bf16[512,2048]{1,0:T(8,128)(2,1)} %collective-permute-done.12.refs_5_.refs_3_), channel_id=1, source_target_pairs={{0,2},{2,0},{4,6},{6,4},{8,10},{10,8},{12,14},{14,12},{16,18},{18,... | collective-permute-start | bytes 6291464 | tf_op jit(solution)/shard_map/ppermute | solution.py:573
  218.1 47.9 %collective-permute-start.16 = (bf16[512,2048]{1,0:T(8,128)(2,1)}, bf16[512,2048]{1,0:T(8,128)(2,1)}, u32[]{:S(2)}, u32[]{:S(2)}) collective-permute-start(bf16[512,2048]{1,0:T(8,128)(2,1)} %bitcast.45.refs_0_.refs_6_), channel_id=1, source_target_pairs={{0,4},{2,6},{4,0},{6,2},{8,12},{10,14},{12,8},{14,10},{16,20},{18,... | collective-permute-start | bytes 6291464 | tf_op jit(solution)/shard_map/ppermute | solution.py:573
  220.4 25.2 %collective-permute-start.13 = (bf16[256,2048]{1,0:T(8,128)(2,1)}, bf16[256,2048]{1,0:T(8,128)(2,1)}, u32[]{:S(2)}, u32[]{:S(2)}) collective-permute-start(bf16[256,2048]{1,0:T(8,128)(2,1)} %collective-permute-done.11.refs_2_), channel_id=1, source_target_pairs={{0,1},{1,0},{2,3},{3,2},{4,5},{5,4},{6,7},{7,6},{8,9},{9,8},{10,11... | collective-permute-start | bytes 3145736 | tf_op jit(solution)/shard_map/ppermute | solution.py:576
  223.0 44.7 %all-to-all-start.6 = ((bf16[4,128,1024]{2,1,0:T(8,128)(2,1)}), bf16[4,128,1024]{2,1,0:T(8,128)(2,1)S(1)}, u32[]{:S(2)}, u32[]{:S(2)}) async-start(bf16[4,128,1024]{2,1,0:T(8,128)(2,1)} %bitcast.127), calls=%async_computation.6 | async-start | bytes 2097152 | tf_op jit(solution)/shard_map/all_to_all | solution.py:579
  226.7 44.8 %collective-permute-start.19 = (bf16[1,256,2048]{2,1,0:T(8,128)(2,1)}, bf16[1,256,2048]{2,1,0:T(8,128)(2,1)}, u32[]{:S(2)}, u32[]{:S(2)}) collective-permute-start(bf16[1,256,2048]{2,1,0:T(8,128)(2,1)} %constant_dynamic-slice_fusion.4), channel_id=1, source_target_pairs={{0,8},{2,10},{4,12},{6,14},{8,0},{10,2},{12,4},{14,6},{16,24},{18,... | collective-permute-start | bytes 3145736 | tf_op jit(solution)/shard_map/ppermute | solution.py:573
  267.7 35.3 %all-to-all-start.5 = ((bf16[4,128,1024]{2,1,0:T(8,128)(2,1)}), bf16[4,128,1024]{2,1,0:T(8,128)(2,1)S(1)}, u32[]{:S(2)}, u32[]{:S(2)}) async-start(bf16[4,128,1024]{2,1,0:T(8,128)(2,1)} %bitcast.47), calls=%async_computation.5 | async-start | bytes 2097152 | tf_op jit(solution)/shard_map/all_to_all | solution.py:579
  271.6 28.2 %collective-permute-start.20 = (bf16[1,256,2048]{2,1,0:T(8,128)(2,1)}, bf16[1,256,2048]{2,1,0:T(8,128)(2,1)}, u32[]{:S(2)}, u32[]{:S(2)}) collective-permute-start(bf16[1,256,2048]{2,1,0:T(8,128)(2,1)} %collective-permute-done.19.in_ref), channel_id=1, source_target_pairs={{0,1},{1,0},{2,3},{3,2},{4,5},{5,4},{6,7},{7,6},{8,9},{9,8},{10,11... | collective-permute-start | bytes 3145736 | tf_op jit(solution)/shard_map/ppermute | solution.py:576
  273.1 29.9 %collective-permute-start.21 = (bf16[512,1024]{1,0:T(8,128)(2,1)S(1)}, bf16[512,1024]{1,0:T(8,128)(2,1)S(1)}, u32[]{:S(2)}, u32[]{:S(2)}) collective-permute-start(bf16[512,1024]{1,0:T(8,128)(2,1)S(1)} %bitcast.111), channel_id=1, source_target_pairs={{0,4},{2,6},{4,0},{6,2},{8,12},{10,14},{12,8},{14,10},{16,20},{18,... | collective-permute-start | bytes 3145736 | tf_op jit(solution)/shard_map/ppermute | solution.py:573
  303.6 25.2 %collective-permute-start.22 = (bf16[512,1024]{1,0:T(8,128)(2,1)S(1)}, bf16[512,1024]{1,0:T(8,128)(2,1)}, u32[]{:S(2)}, u32[]{:S(2)}) collective-permute-start(bf16[512,1024]{1,0:T(8,128)(2,1)S(1)} %bitcast.115), channel_id=1, source_target_pairs={{0,4},{2,6},{4,0},{6,2},{8,12},{10,14},{12,8},{14,10},{16,20},{18,... | collective-permute-start | bytes 3145736 | tf_op jit(solution)/shard_map/ppermute | solution.py:573
  350.3 59.6 %collective-permute-start.30 = (bf16[512,2048]{1,0:T(8,128)(2,1)}, bf16[512,2048]{1,0:T(8,128)(2,1)S(1)}, u32[]{:S(2)}, u32[]{:S(2)}) collective-permute-start(bf16[512,2048]{1,0:T(8,128)(2,1)} %get-tuple-element.218), channel_id=1, source_target_pairs={{0,4},{2,6},{4,0},{6,2},{8,12},{10,14},{12,8},{14,10},{16,20},{18,... | collective-permute-start | bytes 6291464 | tf_op jit(solution)/shard_map/ppermute | solution.py:573
  390.0 25.5 %collective-permute-start.28 = (bf16[256,2048]{1,0:T(8,128)(2,1)}, bf16[256,2048]{1,0:T(8,128)(2,1)S(1)}, u32[]{:S(2)}, u32[]{:S(2)}) collective-permute-start(bf16[256,2048]{1,0:T(8,128)(2,1)} %get-tuple-element.209), channel_id=1, source_target_pairs={{0,8},{2,10},{4,12},{6,14},{8,0},{10,2},{12,4},{14,6},{16,24},{18,... | collective-permute-start | bytes 3145736 | tf_op jit(solution)/shard_map/ppermute | solution.py:573
  392.1 24.9 %collective-permute-start.29 = (bf16[256,2048]{1,0:T(8,128)(2,1)}, bf16[256,2048]{1,0:T(8,128)(2,1)S(1)}, u32[]{:S(2)}, u32[]{:S(2)}) collective-permute-start(bf16[256,2048]{1,0:T(8,128)(2,1)} %get-tuple-element.212), channel_id=1, source_target_pairs={{0,1},{1,0},{2,3},{3,2},{4,5},{5,4},{6,7},{7,6},{8,9},{9,8},{10,11... | collective-permute-start | bytes 3145736 | tf_op jit(solution)/shard_map/ppermute | solution.py:576
  417.0 57.4 %collective-permute-start.34 = (bf16[1024,2048]{1,0:T(8,128)(2,1)}, bf16[1024,2048]{1,0:T(8,128)(2,1)}, u32[]{:S(2)}, u32[]{:S(2)}) collective-permute-start(bf16[1024,2048]{1,0:T(8,128)(2,1)} %shard_map.219), channel_id=1, source_target_pairs={{0,2},{2,0},{4,6},{6,4},{8,10},{10,8},{12,14},{14,12},{16,18},{18,... | collective-permute-start | bytes 12582920 | tf_op jit(solution)/shard_map/ppermute | solution.py:573
  432.0 57.6 %all-to-all-start.7 = ((bf16[4,128,2048]{2,1,0:T(8,128)(2,1)}), bf16[4,128,2048]{2,1,0:T(8,128)(2,1)S(1)}, u32[]{:S(2)}, u32[]{:S(2)}) async-start(bf16[4,128,2048]{2,1,0:T(8,128)(2,1)} %bitcast.51), calls=%async_computation.7 | async-start | bytes 4194304 | tf_op jit(solution)/shard_map/all_to_all | solution.py:579
  441.5 38.8 %collective-permute-start.36 = (bf16[512,1024]{1,0:T(8,128)(2,1)}, bf16[512,1024]{1,0:T(8,128)(2,1)S(1)}, u32[]{:S(2)}, u32[]{:S(2)}) collective-permute-start(bf16[512,1024]{1,0:T(8,128)(2,1)} %get-tuple-element.238), channel_id=1, source_target_pairs={{0,4},{2,6},{4,0},{6,2},{8,12},{10,14},{12,8},{14,10},{16,20},{18,... | collective-permute-start | bytes 3145736 | tf_op jit(solution)/shard_map/ppermute | solution.py:573
  454.5 33.2 %collective-permute-start.37 = (bf16[512,1024]{1,0:T(8,128)(2,1)}, bf16[512,1024]{1,0:T(8,128)(2,1)S(1)}, u32[]{:S(2)}, u32[]{:S(2)}) collective-permute-start(bf16[512,1024]{1,0:T(8,128)(2,1)} %get-tuple-element.240), channel_id=1, source_target_pairs={{0,4},{2,6},{4,0},{6,2},{8,12},{10,14},{12,8},{14,10},{16,20},{18,... | collective-permute-start | bytes 3145736 | tf_op jit(solution)/shard_map/ppermute | solution.py:573
  455.1 34.6 %collective-permute-start.33 = (bf16[256,2048]{1,0:T(8,128)(2,1)S(1)}, bf16[256,2048]{1,0:T(8,128)(2,1)}, u32[]{:S(2)}, u32[]{:S(2)}) collective-permute-start(bf16[256,2048]{1,0:T(8,128)(2,1)S(1)} %copy-done.36), channel_id=1, source_target_pairs={{0,1},{1,0},{2,3},{3,2},{4,5},{5,4},{6,7},{7,6},{8,9},{9,8},{10,11... | collective-permute-start | bytes 3145736 | tf_op jit(solution)/shard_map/ppermute | solution.py:576
  490.9 57.6 %all-to-all-start.8 = ((bf16[4,128,2048]{2,1,0:T(8,128)(2,1)}), bf16[4,128,2048]{2,1,0:T(8,128)(2,1)}, u32[]{:S(2)}, u32[]{:S(2)}) async-start(bf16[4,128,2048]{2,1,0:T(8,128)(2,1)} %bitcast.121), calls=%async_computation.8 | async-start | bytes 4194304 | tf_op jit(solution)/shard_map/all_to_all | solution.py:579
  495.7 26.7 %collective-permute-start.38 = (bf16[512,1024]{1,0:T(8,128)(2,1)}, bf16[512,1024]{1,0:T(8,128)(2,1)S(1)}, u32[]{:S(2)}, u32[]{:S(2)}) collective-permute-start(bf16[512,1024]{1,0:T(8,128)(2,1)} %get-tuple-element.245), channel_id=1, source_target_pairs={{0,4},{2,6},{4,0},{6,2},{8,12},{10,14},{12,8},{14,10},{16,20},{18,... | collective-permute-start | bytes 3145736 | tf_op jit(solution)/shard_map/ppermute | solution.py:573
  497.3 25.1 %collective-permute-start.39 = (bf16[256,2048]{1,0:T(8,128)(2,1)S(1)}, bf16[256,2048]{1,0:T(8,128)(2,1)S(1)}, u32[]{:S(2)}, u32[]{:S(2)}) collective-permute-start(bf16[256,2048]{1,0:T(8,128)(2,1)S(1)} %copy-done.27), channel_id=1, source_target_pairs={{0,1},{1,0},{2,3},{3,2},{4,5},{5,4},{6,7},{7,6},{8,9},{9,8},{10,11... | collective-permute-start | bytes 3145736 | tf_op jit(solution)/shard_map/ppermute | solution.py:576
  522.4 26.1 %collective-permute-start.40 = (bf16[512,1024]{1,0:T(8,128)(2,1)}, bf16[512,1024]{1,0:T(8,128)(2,1)}, u32[]{:S(2)}, u32[]{:S(2)}) collective-permute-start(bf16[512,1024]{1,0:T(8,128)(2,1)} %get-tuple-element.258), channel_id=1, source_target_pairs={{0,4},{2,6},{4,0},{6,2},{8,12},{10,14},{12,8},{14,10},{16,20},{18,... | collective-permute-start | bytes 3145736 | tf_op jit(solution)/shard_map/ppermute | solution.py:573
  522.9 25.6 %collective-permute-start.41 = (bf16[256,2048]{1,0:T(8,128)(2,1)S(1)}, bf16[256,2048]{1,0:T(8,128)(2,1)}, u32[]{:S(2)}, u32[]{:S(2)}) collective-permute-start(bf16[256,2048]{1,0:T(8,128)(2,1)S(1)} %copy-done.29), channel_id=1, source_target_pairs={{0,1},{1,0},{2,3},{3,2},{4,5},{5,4},{6,7},{7,6},{8,9},{9,8},{10,11... | collective-permute-start | bytes 3145736 | tf_op jit(solution)/shard_map/ppermute | solution.py:576
  552.9 53.5 %all-to-all-start.9 = ((bf16[4,128,2048]{2,1,0:T(8,128)(2,1)}), bf16[4,128,2048]{2,1,0:T(8,128)(2,1)S(1)}, u32[]{:S(2)}, u32[]{:S(2)}) async-start(bf16[4,128,2048]{2,1,0:T(8,128)(2,1)} %bitcast.120), calls=%async_computation.9 | async-start | bytes 4194304 | tf_op jit(solution)/shard_map/all_to_all | solution.py:579
  572.2 30.4 %collective-permute-start.44 = (bf16[512,1280]{1,0:T(8,128)(2,1)}, bf16[512,1280]{1,0:T(8,128)(2,1)S(1)}, u32[]{:S(2)}, u32[]{:S(2)}) collective-permute-start(bf16[512,1280]{1,0:T(8,128)(2,1)} %get-tuple-element.273), channel_id=1, source_target_pairs={{0,4},{2,6},{4,0},{6,2},{8,12},{10,14},{12,8},{14,10},{16,20},{18,... | collective-permute-start | bytes 3932168 | tf_op jit(solution)/shard_map/ppermute | solution.py:573
  573.8 46.7 %collective-permute-start.42 = (bf16[256,2048]{1,0:T(8,128)(2,1)}, bf16[256,2048]{1,0:T(8,128)(2,1)}, u32[]{:S(2)}, u32[]{:S(2)}) collective-permute-start(bf16[256,2048]{1,0:T(8,128)(2,1)} %get-tuple-element.262), channel_id=1, source_target_pairs={{0,8},{2,10},{4,12},{6,14},{8,0},{10,2},{12,4},{14,6},{16,24},{18,... | collective-permute-start | bytes 3145736 | tf_op jit(solution)/shard_map/ppermute | solution.py:573
  585.3 37.3 %collective-permute-start.45 = (bf16[256,2048]{1,0:T(8,128)(2,1)}, bf16[256,2048]{1,0:T(8,128)(2,1)}, u32[]{:S(2)}, u32[]{:S(2)}) collective-permute-start(bf16[256,2048]{1,0:T(8,128)(2,1)} %get-tuple-element.275), channel_id=1, source_target_pairs={{0,1},{1,0},{2,3},{3,2},{4,5},{5,4},{6,7},{7,6},{8,9},{9,8},{10,11... | collective-permute-start | bytes 3145736 | tf_op jit(solution)/shard_map/ppermute | solution.py:576
  606.4 35.0 %all-to-all-start.10 = ((bf16[4,128,1280]{2,1,0:T(8,128)(2,1)}), bf16[4,128,1280]{2,1,0:T(8,128)(2,1)S(1)}, u32[]{:S(2)}, u32[]{:S(2)}) async-start(bf16[4,128,1280]{2,1,0:T(8,128)(2,1)} %bitcast.124), calls=%async_computation.10 | async-start | bytes 2621440 | tf_op jit(solution)/shard_map/all_to_all | solution.py:579
  610.0 30.0 %collective-permute-start.54 = (bf16[512,1280]{1,0:T(8,128)(2,1)}, bf16[512,1280]{1,0:T(8,128)(2,1)S(1)}, u32[]{:S(2)}, u32[]{:S(2)}) collective-permute-start(bf16[512,1280]{1,0:T(8,128)(2,1)} %get-tuple-element.291), channel_id=1, source_target_pairs={{0,4},{2,6},{4,0},{6,2},{8,12},{10,14},{12,8},{14,10},{16,20},{18,... | collective-permute-start | bytes 3932168 | tf_op jit(solution)/shard_map/ppermute | solution.py:573
  612.5 33.6 %collective-permute-start.49 = (f32[2048]{0:T(1024)S(1)}, f32[2048]{0:T(1024)S(1)}, u32[]{:S(2)}, u32[]{:S(2)}) collective-permute-start(f32[2048]{0:T(1024)S(1)} %bitcast.129), channel_id=1, source_target_pairs={{0,1},{1,0},{2,3},{3,2},{4,5},{5,4},{6,7},{7,6},{8,9},{9,8},{10,11... | collective-permute-start | bytes 24584 | tf_op jit(solution)/shard_map/ppermute | solution.py:576
  624.7 22.3 %collective-permute-start.46 = (bf16[128,2048]{1,0:T(8,128)(2,1)}, bf16[128,2048]{1,0:T(8,128)(2,1)S(1)}, u32[]{:S(2)}, u32[]{:S(2)}) collective-permute-start(bf16[128,2048]{1,0:T(8,128)(2,1)} %add_convert_fusion.8), channel_id=1, source_target_pairs={{0,1},{1,0},{2,3},{3,2},{4,5},{5,4},{6,7},{7,6},{8,9},{9,8},{10,11... | collective-permute-start | bytes 1572872 | tf_op jit(solution)/shard_map/ppermute | solution.py:576
  626.2 25.4 %collective-permute-start.47 = (bf16[128,2048]{1,0:T(8,128)(2,1)}, bf16[128,2048]{1,0:T(8,128)(2,1)}, u32[]{:S(2)}, u32[]{:S(2)}) collective-permute-start(bf16[128,2048]{1,0:T(8,128)(2,1)} %add_convert_fusion.7), channel_id=1, source_target_pairs={{0,8},{2,10},{4,12},{6,14},{8,0},{10,2},{12,4},{14,6},{16,24},{18,... | collective-permute-start | bytes 1572872 | tf_op jit(solution)/shard_map/ppermute | solution.py:573
  641.4 44.5 %all-to-all-start.11 = ((bf16[4,128,1280]{2,1,0:T(8,128)(2,1)}), bf16[4,128,1280]{2,1,0:T(8,128)(2,1)S(1)}, u32[]{:S(2)}, u32[]{:S(2)}) async-start(bf16[4,128,1280]{2,1,0:T(8,128)(2,1)} %bitcast.123), calls=%async_computation.11 | async-start | bytes 2621440 | tf_op jit(solution)/shard_map/all_to_all | solution.py:579
  655.1 24.1 %collective-permute-start.48 = (bf16[256,2048]{1,0:T(8,128)(2,1)}, bf16[256,2048]{1,0:T(8,128)(2,1)}, u32[]{:S(2)}, u32[]{:S(2)}) collective-permute-start(bf16[256,2048]{1,0:T(8,128)(2,1)} %shard_map.233), channel_id=1, source_target_pairs={{0,1},{1,0},{2,3},{3,2},{4,5},{5,4},{6,7},{7,6},{8,9},{9,8},{10,11... | collective-permute-start | bytes 3145736 | tf_op jit(solution)/shard_map/ppermute | solution.py:576
  (65 other events, 798.9 us)
where the time goes:
time: 696 us; the launch traced here: 690 us
  Pallas kernels  288 us (41%)
  waiting for transfers between devices  241 us (35%)
  starting transfers between devices  103 us (15%)
  other arithmetic  35.3 us (5%)
  local copies, waits for them, and re-layouts  21.3 us (3%)
    pallas_call x37, Pallas kernels, kernel_call(): pl.pallas_call(kernel, grid_spec=pltpu.PrefetchScalarGridSpec(num_scalar_...  288 us
    ppermute x42, waiting for transfers between devices, swap(): return lax.ppermute(array, 'dp', [(i, i ^ bit) for i in range(n)])  136 us
    ppermute x13, waiting for transfers between devices, swap_mp(): return lax.ppermute(array, 'mp', [(0, 1), (1, 0)])  73.9 us
    all_to_all x12, starting transfers between devices, along_z(): lax.all_to_all(array, 'dp', 0, 0, axis_index_groups=z_groups, tiled=True)  53.5 us
    ppermute x42, starting transfers between devices, swap(): return lax.ppermute(array, 'dp', [(i, i ^ bit) for i in range(n)])  32.8 us
    all_to_all x12, waiting for transfers between devices, along_z(): lax.all_to_all(array, 'dp', 0, 0, axis_index_groups=z_groups, tiled=True)  30.8 us
    ppermute x13, starting transfers between devices, swap_mp(): return lax.ppermute(array, 'mp', [(0, 1), (1, 0)])  16.4 us
    concatenate x7, other arithmetic, gather_z(): return along_z(go(jnp.concatenate([first, second, first, second], axis=0)))  15.3 us
  transfers between devices with their start and end apart: 67, of which 29 were waited for; matrix products, arithmetic and copies ran while one was open for 7% of the time, Pallas kernels for 40%

commit v1 on v0

--- a/solution.py
+++ b/solution.py
@@ -41,6 +41,8 @@
     first = len(scalars) + len(ins)
 
     def spec(array, block, place):
+        if block is None:
+            return pl.BlockSpec(memory_space=pl.ANY)
         single = tuple(block) == array.shape or place.__name__ == "fixed"
         mode = pl.Buffered(1) if single and math.prod(grid) > 1 else None
         return pl.BlockSpec(block, place, pipeline_mode=mode)
@@ -321,17 +323,33 @@
     grad_up_ref[...] = (grad * (gate * sigmoid)).astype(BF16)
 
 
-def back_kernel(per_piece, sides, *refs):
+def back_kernel(sides, *refs):
     lefts, refs = refs[:sides], refs[sides:]
-    weights, outs = refs[: sides * PIECES], refs[sides * PIECES :]
+    weights, outs = refs[: sides * PIECES], refs[sides * PIECES : -2]
+    held_ref, sems = refs[-2:]
     rows = outs[0].shape[0]
+
+    def copies(p):
+        return [
+            pltpu.make_async_copy(
+                weights[s * PIECES + p], held_ref.at[p % 2, s], sems.at[p % 2, s]
+            )
+            for s in range(sides)
+        ]
+
     for p in range(PIECES):
 
-        @pl.when(pl.program_id(0) // per_piece == p)
+        @pl.when(pl.program_id(0) == p)
         def _(p=p):
+            for ahead in (0, 1) if p == 0 else (p + 1,):
+                if ahead < PIECES:
+                    for copy in copies(ahead):
+                        copy.start()
+            for copy in copies(p):
+                copy.wait()
             total = None
             for s in range(sides):
-                part = dot(lefts[s][...], weights[s * PIECES + p][...], 1, 1)
+                part = dot(lefts[s][...], held_ref[p % 2, s], 1, 1)
                 total = part if total is None else total + part
             total = total.astype(BF16)
             outs[0][...] = total[:rows]
@@ -349,9 +367,7 @@
 
 
 def times_back(sides, rows):
-    depth = sides[0][1][0].shape[0]
-    columns = min(depth, 512)
-    per_piece = depth // columns
+    depth, count = sides[0][1][0].shape
     ins = []
     for left, pieces, *place in sides:
         at = (0, place[0] if place else 0)
@@ -359,23 +375,22 @@
         def fixed(j, at=at):
             return at
 
-        ins.append((left, (left.shape[0], pieces[0].shape[1]), fixed))
+        ins.append((left, (left.shape[0], count), fixed))
     for _, pieces, *_ in sides:
-        for p, piece in enumerate(pieces):
-
-            def place(j, p=p):
-                return (jnp.clip(j - p * per_piece, 0, per_piece - 1), 0)
-
-            ins.append((piece, (columns, piece.shape[1]), place))
+        ins += [(piece, None, None) for piece in pieces]
     heights = (rows, rows, rows, rows // 2, rows // 2)
     if sides[0][0].shape[0] == 2 * rows:
         heights = (rows, rows)
     return kernel_call(
-        functools.partial(back_kernel, per_piece, len(sides)),
-        (PIECES * per_piece,),
+        functools.partial(back_kernel, len(sides)),
+        (PIECES,),
         ins,
-        [((h, depth * PIECES), BF16, (h, columns), lambda j: (0, j)) for h in heights],
-        time=7 * len(sides) * sides[0][0].shape[1] / 1024,
+        [((h, depth * PIECES), BF16, (h, depth), lambda j: (0, j)) for h in heights],
+        scratch=[
+            pltpu.VMEM((2, len(sides), depth, count), BF16),
+            pltpu.SemaphoreType.DMA((2, len(sides))),
+        ],
+        time=7 * len(sides) * count / 1024,
     )
 
 

time: 696 us -> 694 us (level)
  no operation moved by 1% of the time
where the time goes in v1:
time: 694 us; the launch traced here: 688 us
  Pallas kernels  286 us (41%)
  waiting for transfers between devices  241 us (35%)
  starting transfers between devices  103 us (15%)
  other arithmetic  35.3 us (5%)
  local copies, waits for them, and re-layouts  21.3 us (3%)
    pallas_call x37, Pallas kernels, kernel_call(): pl.pallas_call(kernel, grid_spec=pltpu.PrefetchScalarGridSpec(num_scalar_...  286 us
    ppermute x42, waiting for transfers between devices, swap(): return lax.ppermute(array, 'dp', [(i, i ^ bit) for i in range(n)])  136 us
    ppermute x13, waiting for transfers between devices, swap_mp(): return lax.ppermute(array, 'mp', [(0, 1), (1, 0)])  73.9 us
    all_to_all x12, starting transfers between devices, along_z(): lax.all_to_all(array, 'dp', 0, 0, axis_index_groups=z_groups, tiled=True)  53.5 us
    ppermute x42, starting transfers between devices, swap(): return lax.ppermute(array, 'dp', [(i, i ^ bit) for i in range(n)])  32.8 us
    all_to_all x12, waiting for transfers between devices, along_z(): lax.all_to_all(array, 'dp', 0, 0, axis_index_groups=z_groups, tiled=True)  30.8 us
    ppermute x13, starting transfers between devices, swap_mp(): return lax.ppermute(array, 'mp', [(0, 1), (1, 0)])  16.5 us
    concatenate x7, other arithmetic, gather_z(): return along_z(go(jnp.concatenate([first, second, first, second], axis=0)))  15.3 us
  transfers between devices with their start and end apart: 67, of which 29 were waited for; matrix products, arithmetic and copies ran while one was open for 7% of the time, Pallas kernels for 40%

profile of v1, /device:TPU:0, one launch (start us, length us, event | category | flops | bytes accessed | tf_op | source)
XLA Modules:
  0.0 687.6 jit_solution(17707689176620025445)
XLA Ops:
  2.8 6.4 all-to-all-start
  10.5 5.1 maximum_maximum_fusion
  15.6 16.6 %all-to-all-done = bf16[4,128,896]{2,1,0:T(8,128)(2,1)S(1)} async-done(((bf16[4,128,896]{2,1,0:T(8,128)(2,1)}), bf16[4,128,896]{2,1,0:T(8,128)(2,1)S(1)}, u32[]{:S(2)}, u32[]{:S(2)}) %all-to-all-start) | async-done | bytes 917536 | tf_op jit(solution)/shard_map/all_to_all | solution.py:594
  37.4 5.5 shard_map.203
  46.6 10.7 %collective-permute-done.refs_1_.refs_5_ = bf16[512,896]{1,0:T(8,128)(2,1)} collective-permute-done((bf16[512,896]{1,0:T(8,128)(2,1)S(1)}, bf16[512,896]{1,0:T(8,128)(2,1)}, u32[]{:S(2)}, u32[]{:S(2)}) %collective-permute-start) | collective-permute-done | bytes 917536 | tf_op jit(solution)/shard_map/ppermute | solution.py:588
  61.7 4.7 all-to-all-start.2
  66.4 11.1 %collective-permute-done.3.refs_5_.refs_9_ = bf16[512,768]{1,0:T(8,128)(2,1)} collective-permute-done((bf16[512,768]{1,0:T(8,128)(2,1)S(1)}, bf16[512,768]{1,0:T(8,128)(2,1)}, u32[]{:S(2)}, u32[]{:S(2)}) %collective-permute-start.3) | collective-permute-done | bytes 786464 | tf_op jit(solution)/shard_map/ppermute | solution.py:588
  80.3 11.8 %all-to-all-done.2 = bf16[4,128,1024]{2,1,0:T(8,128)(2,1)S(1)} async-done(((bf16[4,128,1024]{2,1,0:T(8,128)(2,1)}), bf16[4,128,1024]{2,1,0:T(8,128)(2,1)S(1)}, u32[]{:S(2)}, u32[]{:S(2)}) %all-to-all-start.2) | async-done | bytes 1048608 | tf_op jit(solution)/shard_map/all_to_all | solution.py:594
  102.2 14.8 %shard_map.204 = (bf16[512,2048]{1,0:T(8,128)(2,1)}, bf16[512,2048]{1,0:T(8,128)(2,1)}, bf16[512,1536]{1,0:T(8,128)(2,1)}, bf16[512,1024]{1,0:T(8,128)(2,1)}, f32[8,2048]{1,0:T(8,128)}) custom-call(s32[17]{0:T(128)} %concatenate.50.table_ref, bf16[2,256,2048]{2,1,0:T(8,128)(2,1)} %in_ref.5, bf16[512,896]{1,0:T(8,128)(2,1)} %bitcast.103, ...), custom_call_target="tpu_custom_call" | custom-call | flops 1 | bytes 15000 | tf_op jit(solution)/shard_map/pallas_call | solution.py:49
  122.4 7.0 %shard_map.206 = (bf16[256,2048]{1,0:T(8,128)(2,1)}, bf16[256,2048]{1,0:T(8,128)(2,1)}) custom-call(bf16[512,1024]{1,0:T(8,128)(2,1)} %get-tuple-element.266.refs_0_.right_ref, bf16[512,1024]{1,0:T(8,128)(2,1)} %bitcast.98, bf16[512,1024]{1,0:T(8,128)(2,1)} %collective-permute-done.6.refs_2_.refs_1_, bf16[512,1024]{1,0:T(8,128)(2,1)} %copy-done.6, ...), custom_call_target="tpu_custom_call" | custom-call | flops 1 | bytes 7000 | tf_op jit(solution)/shard_map/pallas_call | solution.py:49
  132.7 22.3 %collective-permute-done.9.other_ref = bf16[256,2048]{1,0:T(8,128)(2,1)} collective-permute-done((bf16[256,2048]{1,0:T(8,128)(2,1)}, bf16[256,2048]{1,0:T(8,128)(2,1)}, u32[]{:S(2)}, u32[]{:S(2)}) %collective-permute-start.9) | collective-permute-done | bytes 1048608 | tf_op jit(solution)/shard_map/ppermute | solution.py:591
  155.0 5.1 all-to-all-start.4
  168.8 20.6 %collective-permute-done.10.refs_1_ = bf16[256,2048]{1,0:T(8,128)(2,1)} collective-permute-done((bf16[256,2048]{1,0:T(8,128)(2,1)}, bf16[256,2048]{1,0:T(8,128)(2,1)}, u32[]{:S(2)}, u32[]{:S(2)}) %collective-permute-start.10) | collective-permute-done | bytes 1048608 | tf_op jit(solution)/shard_map/ppermute | solution.py:591
  189.4 28.8 %collective-permute-done.11.refs_2_ = bf16[256,2048]{1,0:T(8,128)(2,1)} collective-permute-done((bf16[256,2048]{1,0:T(8,128)(2,1)}, bf16[256,2048]{1,0:T(8,128)(2,1)}, u32[]{:S(2)}, u32[]{:S(2)}) %collective-permute-start.11) | collective-permute-done | bytes 1048608 | tf_op jit(solution)/shard_map/ppermute | solution.py:588
  229.5 16.8 %collective-permute-done.13.refs_3_ = bf16[256,2048]{1,0:T(8,128)(2,1)} collective-permute-done((bf16[256,2048]{1,0:T(8,128)(2,1)}, bf16[256,2048]{1,0:T(8,128)(2,1)}, u32[]{:S(2)}, u32[]{:S(2)}) %collective-permute-start.13) | collective-permute-done | bytes 1048608 | tf_op jit(solution)/shard_map/ppermute | solution.py:591
  246.3 13.8 %shard_map.208 = (bf16[1024,2048]{1,0:T(8,128)(2,1)}, bf16[1024,2048]{1,0:T(8,128)(2,1)}) custom-call(bf16[256,2048]{1,0:T(8,128)(2,1)} %get-tuple-element.171.refs_0_, bf16[256,2048]{1,0:T(8,128)(2,1)} %collective-permute-done.10.refs_1_, bf16[256,2048]{1,0:T(8,128)(2,1)} %collective-permute-done.11.refs_2_, ...), custom_call_target="tpu_custom_call" | custom-call | flops 1 | bytes 14000 | tf_op jit(solution)/shard_map/pallas_call | solution.py:49
  260.1 6.6 collective-permute-done.16.refs_1_.refs_7_
  285.2 15.3 %shard_map.209 = (bf16[1024,2048]{1,0:T(8,128)(2,1)}, bf16[1024,2048]{1,0:T(8,128)(2,1)}) custom-call(bf16[1024,2048]{1,0:T(8,128)(2,1)} %get-tuple-element.178.all_ref.left_ref, bf16[512,2048]{1,0:T(8,128)(2,1)} %bitcast.45.refs_0_.refs_6_, bf16[512,2048]{1,0:T(8,128)(2,1)} %collective-permute-done.16.refs_1_.refs_7_, ...), custom_call_target="tpu_custom_call" | custom-call | flops 1 | bytes 16000 | tf_op jit(solution)/shard_map/pallas_call | solution.py:49
  309.0 11.1 %shard_map.213 = (bf16[1024,2048]{1,0:T(8,128)(2,1)}, bf16[1024,2048]{1,0:T(8,128)(2,1)}) custom-call(bf16[1024,2048]{1,0:T(8,128)(2,1)} %bitcast.87, bf16[512,1024]{1,0:T(8,128)(2,1)} %bitcast.113, bf16[512,1024]{1,0:T(8,128)(2,1)} %copy-done.16, bf16[512,1024]{1,0:T(8,128)(2,1)} %copy-done.17, bf16[512,1024]{1,0:T(8,128)(2,1)} %copy-done.18, ...), custom_call_target="tpu_custom_call" | custom-call | flops 1 | bytes 9000 | tf_op jit(solution)/shard_map/pallas_call | solution.py:49
  320.1 8.6 %shard_map.214 = bf16[1024,2048]{1,0:T(8,128)(2,1)} custom-call(bf16[1024,2048]{1,0:T(8,128)(2,1)} %bitcast.88, bf16[1024,2048]{1,0:T(8,128)(2,1)} %get-tuple-element.250.right_ref.refs_0_.refs_1_), custom_call_target="tpu_custom_call" | custom-call | flops 1 | bytes 8533 | tf_op jit(solution)/shard_map/pallas_call | solution.py:49
  330.1 8.4 %collective-permute-done.25.refs_2_.refs_8_ = bf16[512,1024]{1,0:T(8,128)(2,1)S(1)} collective-permute-done((bf16[512,1024]{1,0:T(8,128)(2,1)S(1)}, bf16[512,1024]{1,0:T(8,128)(2,1)S(1)}, u32[]{:S(2)}, u32[]{:S(2)}) %collective-permute-start.25) | collective-permute-done | bytes 1048608 | tf_op jit(solution)/shard_map/ppermute | solution.py:588
  342.0 9.0 %shard_map.215 = (bf16[512,2048]{1,0:T(8,128)(2,1)}, bf16[512,2048]{1,0:T(8,128)(2,1)}) custom-call(bf16[1024,2048]{1,0:T(8,128)(2,1)} %bitcast.89, bf16[1024,2048]{1,0:T(8,128)(2,1)} %get-tuple-element.250.right_ref.refs_0_.refs_1_, bf16[1024,2048]{1,0:T(8,128)(2,1)} %copy-done.15), custom_call_target="tpu_custom_call" | custom-call | flops 1 | bytes 8533 | tf_op jit(solution)/shard_map/pallas_call | solution.py:49
  351.5 11.1 %shard_map.216 = (bf16[1024,2048]{1,0:T(8,128)(2,1)}, bf16[1024,2048]{1,0:T(8,128)(2,1)}) custom-call(bf16[1024,2048]{1,0:T(8,128)(2,1)} %bitcast.90, bf16[512,1024]{1,0:T(8,128)(2,1)} %bitcast.117, bf16[512,1024]{1,0:T(8,128)(2,1)} %collective-permute-done.22.refs_1_.refs_7_, ...), custom_call_target="tpu_custom_call", output_to_operand_aliasing={{0}: (7, {}), {1}: (8, {})} | custom-call | flops 1 | bytes 9000 | tf_op jit(solution)/shard_map/pallas_call | solution.py:49
  362.6 25.6 %shard_map.217 = (bf16[256,2048]{1,0:T(8,128)(2,1)}, bf16[256,2048]{1,0:T(8,128)(2,1)}, bf16[256,2048]{1,0:T(8,128)(2,1)}, bf16[128,2048]{1,0:T(8,128)(2,1)}, bf16[128,2048]{1,0:T(8,128)(2,1)}) custom-call(bf16[1024,2048]{1,0:T(8,128)(2,1)} %get-tuple-element.239.refs_0_.right_ref, bf16[1024,2048]{1,0:T(8,128)(2,1)} %get-tuple-element.247.refs_1_.right_ref, ...), custom_call_target="tpu_custom_call" | custom-call | flops 1 | bytes 28000 | tf_op jit(solution)/shard_map/pallas_call | solution.py:49
  390.8 8.5 %shard_map.218 = bf16[1024,2048]{1,0:T(8,128)(2,1)} custom-call(bf16[1024,2048]{1,0:T(8,128)(2,1)} %get-tuple-element.178.all_ref.left_ref, bf16[1024,2048]{1,0:T(8,128)(2,1)} %get-tuple-element.239.refs_0_.right_ref), custom_call_target="tpu_custom_call" | custom-call | flops 1 | bytes 8533 | tf_op jit(solution)/shard_map/pallas_call | solution.py:49
  399.3 8.7 %shard_map.219 = bf16[1024,2048]{1,0:T(8,128)(2,1)} custom-call(bf16[1024,2048]{1,0:T(8,128)(2,1)} %get-tuple-element.178.all_ref.left_ref, bf16[1024,2048]{1,0:T(8,128)(2,1)} %get-tuple-element.247.refs_1_.right_ref), custom_call_target="tpu_custom_call" | custom-call | flops 1 | bytes 8533 | tf_op jit(solution)/shard_map/pallas_call | solution.py:49
  417.3 12.7 %collective-permute-done.31.refs_2_ = bf16[128,2048]{1,0:T(8,128)(2,1)} collective-permute-done((bf16[128,2048]{1,0:T(8,128)(2,1)S(1)}, bf16[128,2048]{1,0:T(8,128)(2,1)}, u32[]{:S(2)}, u32[]{:S(2)}) %collective-permute-start.31) | collective-permute-done | bytes 524320 | tf_op jit(solution)/shard_map/ppermute | solution.py:591
  433.9 5.8 shard_map.223
  441.2 5.5 shard_map.220
  446.7 6.0 shard_map.224
  454.7 17.8 %shard_map.221 = (bf16[512,2048]{1,0:T(8,128)(2,1)}, bf16[512,1536]{1,0:T(8,128)(2,1)}, bf16[256,2048]{1,0:T(8,128)(2,1)}) custom-call(bf16[256,2048]{1,0:T(8,128)(2,1)} %get-tuple-element.223.branch_ref, bf16[512,1024]{1,0:T(8,128)(2,1)} %bitcast.99, bf16[512,1024]{1,0:T(8,128)(2,1)} %collective-permute-done.6.refs_2_.refs_1_, bf16[512,1024]{1,0:T(8,128)(2,1)} %copy-done.6, ...), custom_call_target="tpu_custom_call" | custom-call | flops 1 | bytes 15000 | tf_op jit(solution)/shard_map/pallas_call | solution.py:49
  472.5 5.9 shard_map.222
  478.8 7.1 %collective-permute-done.37 = bf16[512,1024]{1,0:T(8,128)(2,1)S(1)} collective-permute-done((bf16[512,1024]{1,0:T(8,128)(2,1)}, bf16[512,1024]{1,0:T(8,128)(2,1)S(1)}, u32[]{:S(2)}, u32[]{:S(2)}) %collective-permute-start.37) | collective-permute-done | bytes 1048608 | tf_op jit(solution)/shard_map/ppermute | solution.py:588
  489.1 4.8 all-to-all-start.8
  496.9 17.8 %shard_map.225 = (bf16[512,2048]{1,0:T(8,128)(2,1)}, bf16[512,1536]{1,0:T(8,128)(2,1)}, bf16[256,2048]{1,0:T(8,128)(2,1)}) custom-call(bf16[256,2048]{1,0:T(8,128)(2,1)} %collective-permute-done.33.branch_ref, bf16[512,1024]{1,0:T(8,128)(2,1)} %bitcast.100, ...), custom_call_target="tpu_custom_call", output_to_operand_aliasing={{0}: (18, {}), {1}: (19, {})} | custom-call | flops 1 | bytes 15000 | tf_op jit(solution)/shard_map/pallas_call | solution.py:49
  514.7 5.9 shard_map.226
  525.6 5.7 shard_map.229
  531.3 14.5 %shard_map.227 = (bf16[256,2048]{1,0:T(8,128)(2,1)}, bf16[256,2048]{1,0:T(8,128)(2,1)}, bf16[256,2048]{1,0:T(8,128)(2,1)}, bf16[128,2048]{1,0:T(8,128)(2,1)}, bf16[128,2048]{1,0:T(8,128)(2,1)}) custom-call(bf16[1024,2048]{1,0:T(8,128)(2,1)} %get-tuple-element.250.right_ref.refs_0_.refs_1_, bf16[1024,2048]{1,0:T(8,128)(2,1)} %get-tuple-element.250.right_ref.refs_0_.refs_1_, ...), custom_call_target="tpu_custom_call" | custom-call | flops 1 | bytes 14000 | tf_op jit(solution)/shard_map/pallas_call | solution.py:49
  550.3 5.3 all-to-all-start.9
  555.5 5.2 shard_map.230
  560.7 6.2 shard_map.232
  573.8 8.8 %shard_map.235 = (f32[2,256,2048]{2,1,0:T(8,128)}, f32[8,2048]{1,0:T(8,128)}) custom-call(s32[17]{0:T(128)} %concatenate.49.table_ref, bf16[512,2048]{1,0:T(8,128)(2,1)} %get-tuple-element.161.rows_ref.values_ref, bf16[512,2048]{1,0:T(8,128)(2,1)} %get-tuple-element.256.left_ref.passed_ref, bf16[256,2048]{1,0:T(8,128)(2,1)} %get-tuple-element.249.refs_0_, ...), custom_call_target="tpu_custom_call" | custom-call | flops 1 | bytes 5000 | tf_op jit(solution)/shard_map/pallas_call | solution.py:49
  590.8 9.2 %collective-permute-done.44 = bf16[512,1280]{1,0:T(8,128)(2,1)S(1)} collective-permute-done((bf16[512,1280]{1,0:T(8,128)(2,1)}, bf16[512,1280]{1,0:T(8,128)(2,1)S(1)}, u32[]{:S(2)}, u32[]{:S(2)}) %collective-permute-start.44) | collective-permute-done | bytes 1310752 | tf_op jit(solution)/shard_map/ppermute | solution.py:588
  611.3 6.5 collective-permute-done.42.pair_one
  623.4 13.9 %collective-permute-done.54 = bf16[512,1280]{1,0:T(8,128)(2,1)S(1)} collective-permute-done((bf16[512,1280]{1,0:T(8,128)(2,1)}, bf16[512,1280]{1,0:T(8,128)(2,1)S(1)}, u32[]{:S(2)}, u32[]{:S(2)}) %collective-permute-start.54) | collective-permute-done | bytes 1310752 | tf_op jit(solution)/shard_map/ppermute | solution.py:588
  638.7 4.7 all-to-all-start.11
  644.4 4.5 collective-permute-done.47.pair_two
  662.3 10.6 %collective-permute-done.52 = f32[2,2,128]{2,1,0:T(2,128)S(1)} collective-permute-done((f32[2,2,128]{2,1,0:T(2,128)S(1)}, f32[2,2,128]{2,1,0:T(2,128)S(1)}, u32[]{:S(2)}, u32[]{:S(2)}) %collective-permute-start.52) | collective-permute-done | bytes 2080 | tf_op jit(solution)/shard_map/ppermute | solution.py:588
  (270 shorter events, 188.0 us)
Async XLA Ops:
  2.8 29.4 %all-to-all-start = ((bf16[4,128,896]{2,1,0:T(8,128)(2,1)}), bf16[4,128,896]{2,1,0:T(8,128)(2,1)S(1)}, u32[]{:S(2)}, u32[]{:S(2)}) async-start(bf16[4,128,896]{2,1,0:T(8,128)(2,1)} %bitcast.128), calls=%async_computation | async-start | bytes 1835008 | tf_op jit(solution)/shard_map/all_to_all | solution.py:594
  32.2 25.1 %all-to-all-start.1 = ((bf16[4,128,768]{2,1,0:T(8,128)(2,1)}), bf16[4,128,768]{2,1,0:T(8,128)(2,1)S(1)}, u32[]{:S(2)}, u32[]{:S(2)}) async-start(bf16[4,128,768]{2,1,0:T(8,128)(2,1)} %bitcast.37), calls=%async_computation.1 | async-start | bytes 1572864 | tf_op jit(solution)/shard_map/all_to_all | solution.py:594
  35.8 21.5 %collective-permute-start = (bf16[512,896]{1,0:T(8,128)(2,1)S(1)}, bf16[512,896]{1,0:T(8,128)(2,1)}, u32[]{:S(2)}, u32[]{:S(2)}) collective-permute-start(bf16[512,896]{1,0:T(8,128)(2,1)S(1)} %bitcast.101), channel_id=1, source_target_pairs={{0,4},{2,6},{4,0},{6,2},{8,12},{10,14},{12,8},{14,10},{16,20},{18,... | collective-permute-start | bytes 2752520 | tf_op jit(solution)/shard_map/ppermute | solution.py:588
  57.3 20.2 %collective-permute-start.1 = (bf16[512,896]{1,0:T(8,128)(2,1)S(1)}, bf16[512,896]{1,0:T(8,128)(2,1)}, u32[]{:S(2)}, u32[]{:S(2)}) collective-permute-start(bf16[512,896]{1,0:T(8,128)(2,1)S(1)} %bitcast.102), channel_id=1, source_target_pairs={{0,2},{2,0},{4,6},{6,4},{8,10},{10,8},{12,14},{14,12},{16,18},{18,... | collective-permute-start | bytes 2752520 | tf_op jit(solution)/shard_map/ppermute | solution.py:588
  57.4 20.1 %collective-permute-start.2 = (bf16[512,896]{1,0:T(8,128)(2,1)}, bf16[512,896]{1,0:T(8,128)(2,1)}, u32[]{:S(2)}, u32[]{:S(2)}) collective-permute-start(bf16[512,896]{1,0:T(8,128)(2,1)} %collective-permute-done.refs_1_.refs_5_), channel_id=1, source_target_pairs={{0,2},{2,0},{4,6},{6,4},{8,10},{10,8},{12,14},{14,12},{16,18},{18,... | collective-permute-start | bytes 2752520 | tf_op jit(solution)/shard_map/ppermute | solution.py:588
  57.9 19.6 %collective-permute-start.3 = (bf16[512,768]{1,0:T(8,128)(2,1)S(1)}, bf16[512,768]{1,0:T(8,128)(2,1)}, u32[]{:S(2)}, u32[]{:S(2)}) collective-permute-start(bf16[512,768]{1,0:T(8,128)(2,1)S(1)} %bitcast.106), channel_id=1, source_target_pairs={{0,4},{2,6},{4,0},{6,2},{8,12},{10,14},{12,8},{14,10},{16,20},{18,... | collective-permute-start | bytes 2359304 | tf_op jit(solution)/shard_map/ppermute | solution.py:588
  61.7 30.4 %all-to-all-start.2 = ((bf16[4,128,1024]{2,1,0:T(8,128)(2,1)}), bf16[4,128,1024]{2,1,0:T(8,128)(2,1)S(1)}, u32[]{:S(2)}, u32[]{:S(2)}) async-start(bf16[4,128,1024]{2,1,0:T(8,128)(2,1)} %bitcast.125), calls=%async_computation.2 | async-start | bytes 2097152 | tf_op jit(solution)/shard_map/all_to_all | solution.py:594
  92.1 24.8 %collective-permute-start.6 = (bf16[512,1024]{1,0:T(8,128)(2,1)S(1)}, bf16[512,1024]{1,0:T(8,128)(2,1)}, u32[]{:S(2)}, u32[]{:S(2)}) collective-permute-start(bf16[512,1024]{1,0:T(8,128)(2,1)S(1)} %bitcast.96), channel_id=1, source_target_pairs={{0,4},{2,6},{4,0},{6,2},{8,12},{10,14},{12,8},{14,10},{16,20},{18,... | collective-permute-start | bytes 3145736 | tf_op jit(solution)/shard_map/ppermute | solution.py:588
  95.8 59.2 %all-to-all-start.3 = ((bf16[4,128,2048]{2,1,0:T(8,128)(2,1)}), bf16[4,128,2048]{2,1,0:T(8,128)(2,1)S(1)}, u32[]{:S(2)}, u32[]{:S(2)}) async-start(bf16[4,128,2048]{2,1,0:T(8,128)(2,1)} %bitcast.119), calls=%async_computation.3 | async-start | bytes 4194304 | tf_op jit(solution)/shard_map/all_to_all | solution.py:594
  129.4 25.6 %collective-permute-start.9 = (bf16[256,2048]{1,0:T(8,128)(2,1)}, bf16[256,2048]{1,0:T(8,128)(2,1)}, u32[]{:S(2)}, u32[]{:S(2)}) collective-permute-start(bf16[256,2048]{1,0:T(8,128)(2,1)} %get-tuple-element.168), channel_id=1, source_target_pairs={{0,1},{1,0},{2,3},{3,2},{4,5},{5,4},{6,7},{7,6},{8,9},{9,8},{10,11... | collective-permute-start | bytes 3145736 | tf_op jit(solution)/shard_map/ppermute | solution.py:591
  155.0 63.2 %all-to-all-start.4 = ((bf16[4,128,2048]{2,1,0:T(8,128)(2,1)}), bf16[4,128,2048]{2,1,0:T(8,128)(2,1)}, u32[]{:S(2)}, u32[]{:S(2)}) async-start(bf16[4,128,2048]{2,1,0:T(8,128)(2,1)} %bitcast.122), calls=%async_computation.4 | async-start | bytes 4194304 | tf_op jit(solution)/shard_map/all_to_all | solution.py:594
  160.1 58.1 %collective-permute-start.12 = (bf16[512,2048]{1,0:T(8,128)(2,1)S(1)}, bf16[512,2048]{1,0:T(8,128)(2,1)}, u32[]{:S(2)}, u32[]{:S(2)}) collective-permute-start(bf16[512,2048]{1,0:T(8,128)(2,1)S(1)} %bitcast.92), channel_id=1, source_target_pairs={{0,4},{2,6},{4,0},{6,2},{8,12},{10,14},{12,8},{14,10},{16,20},{18,... | collective-permute-start | bytes 6291464 | tf_op jit(solution)/shard_map/ppermute | solution.py:588
  165.3 24.1 %collective-permute-start.10 = (bf16[256,2048]{1,0:T(8,128)(2,1)}, bf16[256,2048]{1,0:T(8,128)(2,1)}, u32[]{:S(2)}, u32[]{:S(2)}) collective-permute-start(bf16[256,2048]{1,0:T(8,128)(2,1)} %get-tuple-element.171.refs_0_), channel_id=1, source_target_pairs={{0,1},{1,0},{2,3},{3,2},{4,5},{5,4},{6,7},{7,6},{8,9},{9,8},{10,11... | collective-permute-start | bytes 3145736 | tf_op jit(solution)/shard_map/ppermute | solution.py:591
  166.8 51.4 %collective-permute-start.11 = (bf16[256,2048]{1,0:T(8,128)(2,1)}, bf16[256,2048]{1,0:T(8,128)(2,1)}, u32[]{:S(2)}, u32[]{:S(2)}) collective-permute-start(bf16[256,2048]{1,0:T(8,128)(2,1)} %get-tuple-element.171.refs_0_), channel_id=1, source_target_pairs={{0,8},{2,10},{4,12},{6,14},{8,0},{10,2},{12,4},{14,6},{16,24},{18,... | collective-permute-start | bytes 3145736 | tf_op jit(solution)/shard_map/ppermute | solution.py:588
  218.2 28.1 %collective-permute-start.14 = (bf16[512,2048]{1,0:T(8,128)(2,1)S(1)}, bf16[512,2048]{1,0:T(8,128)(2,1)}, u32[]{:S(2)}, u32[]{:S(2)}) collective-permute-start(bf16[512,2048]{1,0:T(8,128)(2,1)S(1)} %bitcast.93), channel_id=1, source_target_pairs={{0,2},{2,0},{4,6},{6,4},{8,10},{10,8},{12,14},{14,12},{16,18},{18,... | collective-permute-start | bytes 6291464 | tf_op jit(solution)/shard_map/ppermute | solution.py:588
  218.3 28.0 %collective-permute-start.15 = (bf16[512,2048]{1,0:T(8,128)(2,1)}, bf16[512,2048]{1,0:T(8,128)(2,1)}, u32[]{:S(2)}, u32[]{:S(2)}) collective-permute-start(bf16[512,2048]{1,0:T(8,128)(2,1)} %collective-permute-done.12.refs_5_.refs_3_), channel_id=1, source_target_pairs={{0,2},{2,0},{4,6},{6,4},{8,10},{10,8},{12,14},{14,12},{16,18},{18,... | collective-permute-start | bytes 6291464 | tf_op jit(solution)/shard_map/ppermute | solution.py:588
  218.8 47.9 %collective-permute-start.16 = (bf16[512,2048]{1,0:T(8,128)(2,1)}, bf16[512,2048]{1,0:T(8,128)(2,1)}, u32[]{:S(2)}, u32[]{:S(2)}) collective-permute-start(bf16[512,2048]{1,0:T(8,128)(2,1)} %bitcast.45.refs_0_.refs_6_), channel_id=1, source_target_pairs={{0,4},{2,6},{4,0},{6,2},{8,12},{10,14},{12,8},{14,10},{16,20},{18,... | collective-permute-start | bytes 6291464 | tf_op jit(solution)/shard_map/ppermute | solution.py:588
  221.1 25.2 %collective-permute-start.13 = (bf16[256,2048]{1,0:T(8,128)(2,1)}, bf16[256,2048]{1,0:T(8,128)(2,1)}, u32[]{:S(2)}, u32[]{:S(2)}) collective-permute-start(bf16[256,2048]{1,0:T(8,128)(2,1)} %collective-permute-done.11.refs_2_), channel_id=1, source_target_pairs={{0,1},{1,0},{2,3},{3,2},{4,5},{5,4},{6,7},{7,6},{8,9},{9,8},{10,11... | collective-permute-start | bytes 3145736 | tf_op jit(solution)/shard_map/ppermute | solution.py:591
  223.7 44.7 %all-to-all-start.6 = ((bf16[4,128,1024]{2,1,0:T(8,128)(2,1)}), bf16[4,128,1024]{2,1,0:T(8,128)(2,1)S(1)}, u32[]{:S(2)}, u32[]{:S(2)}) async-start(bf16[4,128,1024]{2,1,0:T(8,128)(2,1)} %bitcast.127), calls=%async_computation.6 | async-start | bytes 2097152 | tf_op jit(solution)/shard_map/all_to_all | solution.py:594
  227.4 44.8 %collective-permute-start.19 = (bf16[1,256,2048]{2,1,0:T(8,128)(2,1)}, bf16[1,256,2048]{2,1,0:T(8,128)(2,1)}, u32[]{:S(2)}, u32[]{:S(2)}) collective-permute-start(bf16[1,256,2048]{2,1,0:T(8,128)(2,1)} %constant_dynamic-slice_fusion.4), channel_id=1, source_target_pairs={{0,8},{2,10},{4,12},{6,14},{8,0},{10,2},{12,4},{14,6},{16,24},{18,... | collective-permute-start | bytes 3145736 | tf_op jit(solution)/shard_map/ppermute | solution.py:588
  268.4 35.4 %all-to-all-start.5 = ((bf16[4,128,1024]{2,1,0:T(8,128)(2,1)}), bf16[4,128,1024]{2,1,0:T(8,128)(2,1)S(1)}, u32[]{:S(2)}, u32[]{:S(2)}) async-start(bf16[4,128,1024]{2,1,0:T(8,128)(2,1)} %bitcast.47), calls=%async_computation.5 | async-start | bytes 2097152 | tf_op jit(solution)/shard_map/all_to_all | solution.py:594
  272.3 28.2 %collective-permute-start.20 = (bf16[1,256,2048]{2,1,0:T(8,128)(2,1)}, bf16[1,256,2048]{2,1,0:T(8,128)(2,1)}, u32[]{:S(2)}, u32[]{:S(2)}) collective-permute-start(bf16[1,256,2048]{2,1,0:T(8,128)(2,1)} %collective-permute-done.19.in_ref), channel_id=1, source_target_pairs={{0,1},{1,0},{2,3},{3,2},{4,5},{5,4},{6,7},{7,6},{8,9},{9,8},{10,11... | collective-permute-start | bytes 3145736 | tf_op jit(solution)/shard_map/ppermute | solution.py:591
  273.9 29.9 %collective-permute-start.21 = (bf16[512,1024]{1,0:T(8,128)(2,1)S(1)}, bf16[512,1024]{1,0:T(8,128)(2,1)S(1)}, u32[]{:S(2)}, u32[]{:S(2)}) collective-permute-start(bf16[512,1024]{1,0:T(8,128)(2,1)S(1)} %bitcast.111), channel_id=1, source_target_pairs={{0,4},{2,6},{4,0},{6,2},{8,12},{10,14},{12,8},{14,10},{16,20},{18,... | collective-permute-start | bytes 3145736 | tf_op jit(solution)/shard_map/ppermute | solution.py:588
  304.3 25.2 %collective-permute-start.22 = (bf16[512,1024]{1,0:T(8,128)(2,1)S(1)}, bf16[512,1024]{1,0:T(8,128)(2,1)}, u32[]{:S(2)}, u32[]{:S(2)}) collective-permute-start(bf16[512,1024]{1,0:T(8,128)(2,1)S(1)} %bitcast.115), channel_id=1, source_target_pairs={{0,4},{2,6},{4,0},{6,2},{8,12},{10,14},{12,8},{14,10},{16,20},{18,... | collective-permute-start | bytes 3145736 | tf_op jit(solution)/shard_map/ppermute | solution.py:588
  351.1 57.0 %collective-permute-start.30 = (bf16[512,2048]{1,0:T(8,128)(2,1)}, bf16[512,2048]{1,0:T(8,128)(2,1)S(1)}, u32[]{:S(2)}, u32[]{:S(2)}) collective-permute-start(bf16[512,2048]{1,0:T(8,128)(2,1)} %get-tuple-element.218), channel_id=1, source_target_pairs={{0,4},{2,6},{4,0},{6,2},{8,12},{10,14},{12,8},{14,10},{16,20},{18,... | collective-permute-start | bytes 6291464 | tf_op jit(solution)/shard_map/ppermute | solution.py:588
  388.2 25.5 %collective-permute-start.28 = (bf16[256,2048]{1,0:T(8,128)(2,1)}, bf16[256,2048]{1,0:T(8,128)(2,1)S(1)}, u32[]{:S(2)}, u32[]{:S(2)}) collective-permute-start(bf16[256,2048]{1,0:T(8,128)(2,1)} %get-tuple-element.209), channel_id=1, source_target_pairs={{0,8},{2,10},{4,12},{6,14},{8,0},{10,2},{12,4},{14,6},{16,24},{18,... | collective-permute-start | bytes 3145736 | tf_op jit(solution)/shard_map/ppermute | solution.py:588
  390.3 24.9 %collective-permute-start.29 = (bf16[256,2048]{1,0:T(8,128)(2,1)}, bf16[256,2048]{1,0:T(8,128)(2,1)S(1)}, u32[]{:S(2)}, u32[]{:S(2)}) collective-permute-start(bf16[256,2048]{1,0:T(8,128)(2,1)} %get-tuple-element.212), channel_id=1, source_target_pairs={{0,1},{1,0},{2,3},{3,2},{4,5},{5,4},{6,7},{7,6},{8,9},{9,8},{10,11... | collective-permute-start | bytes 3145736 | tf_op jit(solution)/shard_map/ppermute | solution.py:591
  415.2 57.4 %collective-permute-start.34 = (bf16[1024,2048]{1,0:T(8,128)(2,1)}, bf16[1024,2048]{1,0:T(8,128)(2,1)}, u32[]{:S(2)}, u32[]{:S(2)}) collective-permute-start(bf16[1024,2048]{1,0:T(8,128)(2,1)} %shard_map.219), channel_id=1, source_target_pairs={{0,2},{2,0},{4,6},{6,4},{8,10},{10,8},{12,14},{14,12},{16,18},{18,... | collective-permute-start | bytes 12582920 | tf_op jit(solution)/shard_map/ppermute | solution.py:588
  430.2 57.6 %all-to-all-start.7 = ((bf16[4,128,2048]{2,1,0:T(8,128)(2,1)}), bf16[4,128,2048]{2,1,0:T(8,128)(2,1)S(1)}, u32[]{:S(2)}, u32[]{:S(2)}) async-start(bf16[4,128,2048]{2,1,0:T(8,128)(2,1)} %bitcast.51), calls=%async_computation.7 | async-start | bytes 4194304 | tf_op jit(solution)/shard_map/all_to_all | solution.py:594
  439.6 38.8 %collective-permute-start.36 = (bf16[512,1024]{1,0:T(8,128)(2,1)}, bf16[512,1024]{1,0:T(8,128)(2,1)S(1)}, u32[]{:S(2)}, u32[]{:S(2)}) collective-permute-start(bf16[512,1024]{1,0:T(8,128)(2,1)} %get-tuple-element.238), channel_id=1, source_target_pairs={{0,4},{2,6},{4,0},{6,2},{8,12},{10,14},{12,8},{14,10},{16,20},{18,... | collective-permute-start | bytes 3145736 | tf_op jit(solution)/shard_map/ppermute | solution.py:588
  452.7 33.2 %collective-permute-start.37 = (bf16[512,1024]{1,0:T(8,128)(2,1)}, bf16[512,1024]{1,0:T(8,128)(2,1)S(1)}, u32[]{:S(2)}, u32[]{:S(2)}) collective-permute-start(bf16[512,1024]{1,0:T(8,128)(2,1)} %get-tuple-element.240), channel_id=1, source_target_pairs={{0,4},{2,6},{4,0},{6,2},{8,12},{10,14},{12,8},{14,10},{16,20},{18,... | collective-permute-start | bytes 3145736 | tf_op jit(solution)/shard_map/ppermute | solution.py:588
  453.2 34.6 %collective-permute-start.33 = (bf16[256,2048]{1,0:T(8,128)(2,1)S(1)}, bf16[256,2048]{1,0:T(8,128)(2,1)}, u32[]{:S(2)}, u32[]{:S(2)}) collective-permute-start(bf16[256,2048]{1,0:T(8,128)(2,1)S(1)} %copy-done.36), channel_id=1, source_target_pairs={{0,1},{1,0},{2,3},{3,2},{4,5},{5,4},{6,7},{7,6},{8,9},{9,8},{10,11... | collective-permute-start | bytes 3145736 | tf_op jit(solution)/shard_map/ppermute | solution.py:591
  489.1 56.8 %all-to-all-start.8 = ((bf16[4,128,2048]{2,1,0:T(8,128)(2,1)}), bf16[4,128,2048]{2,1,0:T(8,128)(2,1)}, u32[]{:S(2)}, u32[]{:S(2)}) async-start(bf16[4,128,2048]{2,1,0:T(8,128)(2,1)} %bitcast.121), calls=%async_computation.8 | async-start | bytes 4194304 | tf_op jit(solution)/shard_map/all_to_all | solution.py:594
  493.9 26.7 %collective-permute-start.38 = (bf16[512,1024]{1,0:T(8,128)(2,1)}, bf16[512,1024]{1,0:T(8,128)(2,1)S(1)}, u32[]{:S(2)}, u32[]{:S(2)}) collective-permute-start(bf16[512,1024]{1,0:T(8,128)(2,1)} %get-tuple-element.245), channel_id=1, source_target_pairs={{0,4},{2,6},{4,0},{6,2},{8,12},{10,14},{12,8},{14,10},{16,20},{18,... | collective-permute-start | bytes 3145736 | tf_op jit(solution)/shard_map/ppermute | solution.py:588
  495.5 25.1 %collective-permute-start.39 = (bf16[256,2048]{1,0:T(8,128)(2,1)S(1)}, bf16[256,2048]{1,0:T(8,128)(2,1)S(1)}, u32[]{:S(2)}, u32[]{:S(2)}) collective-permute-start(bf16[256,2048]{1,0:T(8,128)(2,1)S(1)} %copy-done.27), channel_id=1, source_target_pairs={{0,1},{1,0},{2,3},{3,2},{4,5},{5,4},{6,7},{7,6},{8,9},{9,8},{10,11... | collective-permute-start | bytes 3145736 | tf_op jit(solution)/shard_map/ppermute | solution.py:591
  520.6 25.3 %collective-permute-start.40 = (bf16[512,1024]{1,0:T(8,128)(2,1)}, bf16[512,1024]{1,0:T(8,128)(2,1)}, u32[]{:S(2)}, u32[]{:S(2)}) collective-permute-start(bf16[512,1024]{1,0:T(8,128)(2,1)} %get-tuple-element.258), channel_id=1, source_target_pairs={{0,4},{2,6},{4,0},{6,2},{8,12},{10,14},{12,8},{14,10},{16,20},{18,... | collective-permute-start | bytes 3145736 | tf_op jit(solution)/shard_map/ppermute | solution.py:588
  521.1 24.8 %collective-permute-start.41 = (bf16[256,2048]{1,0:T(8,128)(2,1)S(1)}, bf16[256,2048]{1,0:T(8,128)(2,1)}, u32[]{:S(2)}, u32[]{:S(2)}) collective-permute-start(bf16[256,2048]{1,0:T(8,128)(2,1)S(1)} %copy-done.29), channel_id=1, source_target_pairs={{0,1},{1,0},{2,3},{3,2},{4,5},{5,4},{6,7},{7,6},{8,9},{9,8},{10,11... | collective-permute-start | bytes 3145736 | tf_op jit(solution)/shard_map/ppermute | solution.py:591
  550.3 53.5 %all-to-all-start.9 = ((bf16[4,128,2048]{2,1,0:T(8,128)(2,1)}), bf16[4,128,2048]{2,1,0:T(8,128)(2,1)S(1)}, u32[]{:S(2)}, u32[]{:S(2)}) async-start(bf16[4,128,2048]{2,1,0:T(8,128)(2,1)} %bitcast.120), calls=%async_computation.9 | async-start | bytes 4194304 | tf_op jit(solution)/shard_map/all_to_all | solution.py:594
  569.6 30.5 %collective-permute-start.44 = (bf16[512,1280]{1,0:T(8,128)(2,1)}, bf16[512,1280]{1,0:T(8,128)(2,1)S(1)}, u32[]{:S(2)}, u32[]{:S(2)}) collective-permute-start(bf16[512,1280]{1,0:T(8,128)(2,1)} %get-tuple-element.273), channel_id=1, source_target_pairs={{0,4},{2,6},{4,0},{6,2},{8,12},{10,14},{12,8},{14,10},{16,20},{18,... | collective-permute-start | bytes 3932168 | tf_op jit(solution)/shard_map/ppermute | solution.py:588
  571.2 46.5 %collective-permute-start.42 = (bf16[256,2048]{1,0:T(8,128)(2,1)}, bf16[256,2048]{1,0:T(8,128)(2,1)}, u32[]{:S(2)}, u32[]{:S(2)}) collective-permute-start(bf16[256,2048]{1,0:T(8,128)(2,1)} %get-tuple-element.262), channel_id=1, source_target_pairs={{0,8},{2,10},{4,12},{6,14},{8,0},{10,2},{12,4},{14,6},{16,24},{18,... | collective-permute-start | bytes 3145736 | tf_op jit(solution)/shard_map/ppermute | solution.py:588
  582.6 37.2 %collective-permute-start.45 = (bf16[256,2048]{1,0:T(8,128)(2,1)}, bf16[256,2048]{1,0:T(8,128)(2,1)}, u32[]{:S(2)}, u32[]{:S(2)}) collective-permute-start(bf16[256,2048]{1,0:T(8,128)(2,1)} %get-tuple-element.275), channel_id=1, source_target_pairs={{0,1},{1,0},{2,3},{3,2},{4,5},{5,4},{6,7},{7,6},{8,9},{9,8},{10,11... | collective-permute-start | bytes 3145736 | tf_op jit(solution)/shard_map/ppermute | solution.py:591
  603.8 35.0 %all-to-all-start.10 = ((bf16[4,128,1280]{2,1,0:T(8,128)(2,1)}), bf16[4,128,1280]{2,1,0:T(8,128)(2,1)S(1)}, u32[]{:S(2)}, u32[]{:S(2)}) async-start(bf16[4,128,1280]{2,1,0:T(8,128)(2,1)} %bitcast.124), calls=%async_computation.10 | async-start | bytes 2621440 | tf_op jit(solution)/shard_map/all_to_all | solution.py:594
  607.3 30.0 %collective-permute-start.54 = (bf16[512,1280]{1,0:T(8,128)(2,1)}, bf16[512,1280]{1,0:T(8,128)(2,1)S(1)}, u32[]{:S(2)}, u32[]{:S(2)}) collective-permute-start(bf16[512,1280]{1,0:T(8,128)(2,1)} %get-tuple-element.291), channel_id=1, source_target_pairs={{0,4},{2,6},{4,0},{6,2},{8,12},{10,14},{12,8},{14,10},{16,20},{18,... | collective-permute-start | bytes 3932168 | tf_op jit(solution)/shard_map/ppermute | solution.py:588
  609.8 33.6 %collective-permute-start.49 = (f32[2048]{0:T(1024)S(1)}, f32[2048]{0:T(1024)S(1)}, u32[]{:S(2)}, u32[]{:S(2)}) collective-permute-start(f32[2048]{0:T(1024)S(1)} %bitcast.129), channel_id=1, source_target_pairs={{0,1},{1,0},{2,3},{3,2},{4,5},{5,4},{6,7},{7,6},{8,9},{9,8},{10,11... | collective-permute-start | bytes 24584 | tf_op jit(solution)/shard_map/ppermute | solution.py:591
  622.0 22.4 %collective-permute-start.46 = (bf16[128,2048]{1,0:T(8,128)(2,1)}, bf16[128,2048]{1,0:T(8,128)(2,1)S(1)}, u32[]{:S(2)}, u32[]{:S(2)}) collective-permute-start(bf16[128,2048]{1,0:T(8,128)(2,1)} %add_convert_fusion.8), channel_id=1, source_target_pairs={{0,1},{1,0},{2,3},{3,2},{4,5},{5,4},{6,7},{7,6},{8,9},{9,8},{10,11... | collective-permute-start | bytes 1572872 | tf_op jit(solution)/shard_map/ppermute | solution.py:591
  623.4 25.5 %collective-permute-start.47 = (bf16[128,2048]{1,0:T(8,128)(2,1)}, bf16[128,2048]{1,0:T(8,128)(2,1)}, u32[]{:S(2)}, u32[]{:S(2)}) collective-permute-start(bf16[128,2048]{1,0:T(8,128)(2,1)} %add_convert_fusion.7), channel_id=1, source_target_pairs={{0,8},{2,10},{4,12},{6,14},{8,0},{10,2},{12,4},{14,6},{16,24},{18,... | collective-permute-start | bytes 1572872 | tf_op jit(solution)/shard_map/ppermute | solution.py:588
  638.7 44.5 %all-to-all-start.11 = ((bf16[4,128,1280]{2,1,0:T(8,128)(2,1)}), bf16[4,128,1280]{2,1,0:T(8,128)(2,1)S(1)}, u32[]{:S(2)}, u32[]{:S(2)}) async-start(bf16[4,128,1280]{2,1,0:T(8,128)(2,1)} %bitcast.123), calls=%async_computation.11 | async-start | bytes 2621440 | tf_op jit(solution)/shard_map/all_to_all | solution.py:594
  652.4 24.1 %collective-permute-start.48 = (bf16[256,2048]{1,0:T(8,128)(2,1)}, bf16[256,2048]{1,0:T(8,128)(2,1)}, u32[]{:S(2)}, u32[]{:S(2)}) collective-permute-start(bf16[256,2048]{1,0:T(8,128)(2,1)} %shard_map.233), channel_id=1, source_target_pairs={{0,1},{1,0},{2,3},{3,2},{4,5},{5,4},{6,7},{7,6},{8,9},{9,8},{10,11... | collective-permute-start | bytes 3145736 | tf_op jit(solution)/shard_map/ppermute | solution.py:591
  (65 other events, 798.7 us)
